TPU v7x, 32 devices: a whole 2x2x4 slice. The times are simulated.
32 devices in a mesh: rx: 8 (over z, x), ry: 4 (over y, core).
Axes of the slice: x: 2, y: 2, z: 4, core: 2. Of those that a mesh axis runs over, the one named last changes fastest.
Arguments:
- cell_input: bfloat16 [32, 16, 64, 128], P('rx', 'ry'), may hold values from -6 to 6
- w_filter: bfloat16 [2, 32, 32], replicated, may hold values from -0.75 to 0.75
- w_gate: bfloat16 [2, 32, 32], replicated, may hold values from -0.75 to 0.75
- bias_filter: float32 [32], replicated, may hold values from -3 to 3
- bias_gate: float32 [32], replicated, may hold values from -3 to 3
- adjacency: bfloat16 [32, 16, 5, 4096], P('rx', 'ry'), may hold values from -0.3125 to 0.3125
- out_block: int32 [8, 4, 12], P('rx', 'ry'), may hold values from 0 to 15
- out_dev: int32 [8, 4, 12, 1], P('rx', 'ry'), may hold values from 0 to 7; in each aligned block of 12 rows (0 to 11, 12 to 23, ..., all dimensions but the last counted through in order) at most 2 rows name the same one
- out_target: int32 [8, 4, 12], P('rx', 'ry'), may hold values from 0 to 15
- out_tiles: bfloat16 [8, 4, 12, 4096], P('rx', 'ry'), may hold values from -0.75 to 0.75
- w_mix: bfloat16 [3, 32, 32], replicated, may hold values from -0.625 to 0.625
- bias_mix: float32 [32], replicated, may hold values from -3 to 3
Outputs:
- layer_output: bfloat16 [32, 16, 64, 128], P('rx', 'ry')
Inputs may be any that keep to these rules, and one draw needn't show every extreme that they name: `out_dev`: among the 12 edges of one region no destination region row appears more than 2 times, and in some regions one appears exactly 2 times.
All inputs are finite; a program needn't handle non-finite values.
Results may differ from a plain program's by a relative error of at most 0.0045.
Values may be sent and summed in bfloat16 or wider, within the bound.
A program may use at most 64 MiB of HBM per device.

v0:
```python
import jax
import jax.numpy as jnp
from jax import lax
from jax.sharding import PartitionSpec as P

DILATION_STEP = 2
CAP = 2


def with_halo(array, sides, width):
    for axis, dim in sides:
        size, length = (lax.axis_size(axis), array.shape[dim])
        up = [(i, (i + 1) % size) for i in range(size - 1)]
        down = [(j, i) for i, j in up]
        last = lax.slice_in_dim(array, length - width, length, axis=dim)
        leading = lax.slice_in_dim(array, 0, width, axis=dim)
        before = lax.ppermute(last, axis, up)
        after = lax.ppermute(leading, axis, down)
        array = jnp.concatenate([before, array, after], axis=dim)
    return array


def group_eye(channels):
    group_members = 128 // channels
    input_signals = jnp.arange(group_members, dtype=jnp.int32)[:, None]
    output_signals = jnp.arange(group_members, dtype=jnp.int32)[None, :]
    return (input_signals, output_signals)


def time_tables(w_filter, w_gate, channels):
    group_members = 128 // channels
    input_signals, output_signals = group_eye(channels)
    diagonal = (input_signals == output_signals).astype(jnp.float32)
    within_group = (input_signals == output_signals - DILATION_STEP).astype(jnp.float32)
    across_groups = (input_signals == output_signals - DILATION_STEP + group_members).astype(
        jnp.float32
    )
    filter_taps = w_filter.astype(jnp.float32)
    gate_taps = w_gate.astype(jnp.float32)
    current_tab = jnp.concatenate(
        [
            jnp.kron(diagonal, filter_taps[1]) + jnp.kron(within_group, filter_taps[0]),
            jnp.kron(diagonal, gate_taps[1]) + jnp.kron(within_group, gate_taps[0]),
        ],
        axis=1,
    )
    earlier_tab = jnp.concatenate(
        [jnp.kron(across_groups, filter_taps[0]), jnp.kron(across_groups, gate_taps[0])], axis=1
    )
    return (current_tab.astype(jnp.bfloat16), earlier_tab.astype(jnp.bfloat16))


def gated_units(cell_input, current_tab, earlier_tab, bias_filter, bias_gate):
    block_rows, block_cols, block_size, features = cell_input.shape
    group_members = 128 // bias_filter.shape[0]
    grouped = cell_input.reshape(block_rows * block_cols * block_size, features // 128, 128)
    shifted = jnp.concatenate([jnp.zeros_like(grouped), grouped[:, :-1]], axis=1)
    pre_both = jnp.einsum("ngk,kj->ngj", grouped, current_tab, preferred_element_type=jnp.float32)
    pre_both = pre_both + jnp.einsum(
        "ngk,kj->ngj", shifted, earlier_tab, preferred_element_type=jnp.float32
    )
    filter_bias = jnp.tile(bias_filter, group_members)
    gate_bias = jnp.tile(bias_gate, group_members)
    gated = jnp.tanh(pre_both[..., :128] + filter_bias) * jax.nn.sigmoid(
        pre_both[..., 128:] + gate_bias
    )
    return gated.astype(jnp.bfloat16).reshape(cell_input.shape)


def block_stencil(padded, tiles):
    neighbours = (
        padded[1:-1, 1:-1],
        padded[:-2, 1:-1],
        padded[2:, 1:-1],
        padded[1:-1, :-2],
        padded[1:-1, 2:],
    )
    stencil_sum = jnp.einsum(
        "ijab,ijbf->ijaf", tiles[:, :, 0], neighbours[0], preferred_element_type=jnp.float32
    )
    for offset in range(1, 5):
        stencil_sum = stencil_sum + jnp.einsum(
            "ijab,ijbf->ijaf",
            tiles[:, :, offset],
            neighbours[offset],
            preferred_element_type=jnp.float32,
        )
    return stencil_sum


def fetch_border(signal):
    return with_halo(signal, (("rx", 0), ("ry", 1)), 1)


def local_terms(signal, adjacency):
    block_size = signal.shape[2]
    tiles = adjacency.reshape(adjacency.shape[0], adjacency.shape[1], 5, block_size, block_size)
    bordered = fetch_border(signal)
    stencil_sum = block_stencil(bordered, tiles)
    return stencil_sum


def send_layout(out_block, out_dev, out_target, out_tiles, senders):
    destinations = out_dev.reshape(-1)
    sources = out_block.reshape(-1)
    targets = out_target.reshape(-1)
    edge_count = destinations.shape[0]
    edge_tiles = out_tiles.reshape(edge_count, out_tiles.shape[-1])
    owners = jnp.arange(senders, dtype=jnp.int32)
    dest_hits = (destinations[:, None] == owners[None, :]).astype(jnp.int32)
    edge_ranks = jnp.sum((jnp.cumsum(dest_hits, axis=0) - 1) * dest_hits, axis=1)
    slot_ids = jnp.arange(CAP, dtype=jnp.int32)
    select = dest_hits[:, :, None] * (edge_ranks[:, None, None] == slot_ids[None, None, :]).astype(
        jnp.int32
    )
    select = select.astype(jnp.bfloat16)
    tile_buf = jnp.einsum(
        "edc,ek->dck", select, edge_tiles, preferred_element_type=jnp.float32
    ).astype(jnp.bfloat16)
    target_buf = (
        jnp.einsum("edc,e->dc", select.astype(jnp.float32), (targets + 1).astype(jnp.float32)) - 1.0
    )
    return (select, sources, tile_buf, target_buf.astype(jnp.bfloat16))


def diffuse(signal, adjacency, layout):
    select, sources, tile_buf, target_buf = layout
    block_rows, block_cols, block_size, features = signal.shape
    nblocks = block_rows * block_cols
    near_sum = local_terms(signal, adjacency)
    flat_blocks = signal.reshape(nblocks, block_size, features)
    picked = flat_blocks[sources]
    block_buf = jnp.einsum(
        "edc,eaf->dcaf", select, picked, preferred_element_type=jnp.float32
    ).astype(jnp.bfloat16)
    recv_blocks, recv_tiles, recv_targets = (
        lax.all_to_all(block_buf, "rx", split_axis=0, concat_axis=0, tiled=True),
        lax.all_to_all(tile_buf, "rx", split_axis=0, concat_axis=0, tiled=True),
        lax.all_to_all(target_buf, "rx", split_axis=0, concat_axis=0, tiled=True),
    )
    square_tiles = recv_tiles.reshape(
        recv_tiles.shape[0], recv_tiles.shape[1], block_size, block_size
    )
    products = jnp.einsum(
        "scab,scbf->scaf", square_tiles, recv_blocks, preferred_element_type=jnp.float32
    )
    block_ids = jnp.arange(nblocks, dtype=jnp.int32).astype(jnp.float32)
    onehot = (recv_targets.astype(jnp.float32)[None, :, :] == block_ids[:, None, None]).astype(
        jnp.float32
    )
    far_sum = jnp.einsum("nsc,scaf->naf", onehot, products, precision=lax.Precision.HIGHEST)
    return near_sum + far_sum.reshape(signal.shape)


def local(
    cell_input,
    w_filter,
    w_gate,
    bias_filter,
    bias_gate,
    adjacency,
    out_block,
    out_dev,
    out_target,
    out_tiles,
    w_mix,
    bias_mix,
):
    channels = w_filter.shape[1]
    current_tab, earlier_tab = time_tables(w_filter, w_gate, channels)
    gated = gated_units(cell_input, current_tab, earlier_tab, bias_filter, bias_gate)
    layout = send_layout(out_block, out_dev, out_target, out_tiles, lax.axis_size("rx"))
    first_hop = diffuse(gated, adjacency, layout).astype(jnp.bfloat16)
    second_hop = diffuse(first_hop, adjacency, layout)
    input_signals, output_signals = group_eye(channels)
    diagonal = (input_signals == output_signals).astype(jnp.float32)
    mix_weights = w_mix.astype(jnp.float32)
    table_zero = jnp.kron(diagonal, mix_weights[0]).astype(jnp.bfloat16)
    table_one = jnp.kron(diagonal, mix_weights[1]).astype(jnp.bfloat16)
    table_two = jnp.kron(diagonal, mix_weights[2])
    block_rows, block_cols, block_size, features = cell_input.shape
    grouped_shape = (block_rows * block_cols * block_size, features // 128, 128)
    mixture = jnp.einsum(
        "ngk,kj->ngj", gated.reshape(grouped_shape), table_zero, preferred_element_type=jnp.float32
    )
    mixture = mixture + jnp.einsum(
        "ngk,kj->ngj",
        first_hop.reshape(grouped_shape),
        table_one,
        preferred_element_type=jnp.float32,
    )
    mixture = mixture + jnp.einsum(
        "ngk,kj->ngj", second_hop.reshape(grouped_shape), table_two, precision=lax.Precision.HIGHEST
    )
    mixture = mixture + jnp.tile(bias_mix, 128 // channels)
    output_sum = cell_input.astype(jnp.float32) + mixture.reshape(cell_input.shape)
    return output_sum.astype(jnp.bfloat16)


def solution(mesh):
    in_specs = (
        P("rx", "ry", None, None),
        P(),
        P(),
        P(),
        P(),
        P("rx", "ry", None, None),
        P("rx", "ry", None),
        P("rx", "ry", None, None),
        P("rx", "ry", None),
        P("rx", "ry", None, None),
        P(),
        P(),
    )
    out_specs = P("rx", "ry", None, None)
    return jax.shard_map(local, mesh=mesh, in_specs=in_specs, out_specs=out_specs, check_vma=False)
```

profile of v0, /device:TPU:1, one launch (start us, length us, event | category | flops | bytes accessed | tf_op | source)
XLA Modules:
  0.0 91.2 jit_solution(12563351744988752647)
XLA Ops:
  3.0 6.4 %all-to-all-start = ((bf16[8,1,2]{2,1,0:T(2,128)(2,1)}), bf16[8,1,2]{2,1,0:T(2,128)(2,1)S(1)}, u32[]{:S(2)}, u32[]{:S(2)}) async-start(bf16[8,1,2]{2,1,0:T(2,128)(2,1)} %copy.86), calls=%async_computation | async-start | bytes 8192 | tf_op jit(solution)/shard_map/all_to_all | solution.py:139
  15.9 1.3 %collective-permute-start.1 = (bf16[1,4,64,128]{3,2,1,0:T(8,128)(2,1)}, bf16[1,4,64,128]{3,2,1,0:T(8,128)(2,1)}, u32[]{:S(2)}, u32[]{:S(2)}) collective-permute-start(bf16[1,4,64,128]{3,2,1,0:T(8,128)(2,1)} %bitcast.13), channel_id=1, source_target_pairs={{4,0},{8,4},{12,8},{16,12},{20,16},{24,20},{28,24},{5,1},{9,5},{13... | collective-permute-start | bytes 196616 | tf_op jit(solution)/shard_map/ppermute | solution.py:18
  17.9 4.6 %collective-permute-start = (bf16[1,4,64,128]{3,2,1,0:T(8,128)(2,1)}, bf16[1,4,64,128]{3,2,1,0:T(8,128)(2,1)}, u32[]{:S(2)}, u32[]{:S(2)}) collective-permute-start(bf16[1,4,64,128]{3,2,1,0:T(8,128)(2,1)} %bitcast.11), channel_id=1, source_target_pairs={{0,4},{4,8},{8,12},{12,16},{16,20},{20,24},{24,28},{1,5},{5,9},{9,... | collective-permute-start | bytes 196616 | tf_op jit(solution)/shard_map/ppermute | solution.py:17
  25.2 1.0 %reshape.312 = bf16[4,4,5,64,64]{4,3,1,0,2:T(8,128)(2,1)S(1)} reshape(bf16[4,4,5,4096]{3,1,0,2:T(4,128)(2,1)S(1)} %copy.83) | data formatting | bytes 1310720 | tf_op jit(solution)/shard_map/reshape | solution.py:97
  28.7 1.0 %fusion.35 = f32[1024,128]{1,0:T(8,128)} fusion(bf16[128,128]{1,0:T(8,128)(2,1)S(1)} %convert_element_type.148, bf16[1024,1,128]{0,2,1:T(8,128)(2,1)S(1)} %fusion.20), kind=kOutput, calls=%fused_computation.73 | convolution fusion | flops 33554432 | bytes 819200 | tf_op jit(solution)/shard_map/ngk,kj->ngj/dot_general | solution.py:183
  30.7 4.8 %all-to-all-start.1 = ((bf16[8,2,4096]{2,1,0:T(2,128)(2,1)}), bf16[8,2,4096]{2,1,0:T(2,128)(2,1)S(1)}, u32[]{:S(2)}, u32[]{:S(2)}) async-start(bf16[8,2,4096]{2,1,0:T(2,128)(2,1)} %copy.88), calls=%async_computation.1 | async-start | bytes 262144 | tf_op jit(solution)/shard_map/all_to_all | solution.py:138
  35.6 1.4 %pad_maximum_fusion.37 = (bf16[6,1,64,128]{3,2,1,0:T(8,128)(2,1)S(1)}, bf16[6,1,64,128]{3,2,1,0:T(8,128)(2,1)}) fusion(bf16[1,4,64,128]{3,2,1,0:T(8,128)(2,1)} %collective-permute-done.1, bf16[4,4,64,128]{3,2,1,0:T(8,128)(2,1)S(1)} %bitcast.130, bf16[1,4,64,128]{3,2,1,0:T(8,128)(2,1)} %collective-permute-done), kind=kLoop, calls=%fused_computation.94 | loop fusion | flops 196608 | bytes 589824 | tf_op jit(solution)/shard_map/slice | solution.py:15
  37.1 5.1 %collective-permute-start.2 = (bf16[6,1,64,128]{3,2,1,0:T(8,128)(2,1)S(1)}, bf16[6,1,64,128]{3,2,1,0:T(8,128)(2,1)}, u32[]{:S(2)}, u32[]{:S(2)}) collective-permute-start(bf16[6,1,64,128]{3,2,1,0:T(8,128)(2,1)S(1)} %get-tuple-element.7), channel_id=1, source_target_pairs={{0,1},{1,2},{2,3},{4,5},{5,6},{6,7},{8,9},{9,10},{10,11},{12,13},{... | collective-permute-start | bytes 294920 | tf_op jit(solution)/shard_map/ppermute | solution.py:17
  42.2 1.9 %collective-permute-start.3 = (bf16[6,1,64,128]{3,2,1,0:T(8,128)(2,1)}, bf16[6,1,64,128]{3,2,1,0:T(8,128)(2,1)}, u32[]{:S(2)}, u32[]{:S(2)}) collective-permute-start(bf16[6,1,64,128]{3,2,1,0:T(8,128)(2,1)} %get-tuple-element.8), channel_id=1, source_target_pairs={{1,0},{2,1},{3,2},{5,4},{6,5},{7,6},{9,8},{10,9},{11,10},{13,12},{... | collective-permute-start | bytes 294920 | tf_op jit(solution)/shard_map/ppermute | solution.py:18
  44.1 1.1 %convolution_add_fusion.4 = f32[4,4,128,64]{2,3,1,0:T(8,128)S(1)} fusion(f32[4,4,128,64]{2,3,1,0:T(8,128)S(1)} %fusion.39, bf16[4,4,64,128]{3,2,1,0:T(8,128)(2,1)S(1)} %bitcast.131, bf16[1,4,64,128]{3,2,1,0:T(8,128)(2,1)} %collective-permute-done, bf16[4,4,5,64,64]{4,3,1,0,2:T(8,128)(2,1)S(1)} %reshape.312), kind=kOutput, calls=%fused_computation.20 | convolution fusion | flops 17432576 | bytes 1638400 | tf_op jit(solution)/shard_map/ijab,ijbf->ijaf/dot_general | solution.py:82
  45.2 5.7 %all-to-all-start.2 = ((bf16[8,2,64,128]{3,2,1,0:T(8,128)(2,1)}), bf16[8,2,64,128]{3,2,1,0:T(8,128)(2,1)S(1)}, u32[]{:S(2)}, u32[]{:S(2)}) async-start(bf16[8,2,64,128]{3,2,1,0:T(8,128)(2,1)} %copy.91), calls=%async_computation.2 | async-start | bytes 524288 | tf_op jit(solution)/shard_map/all_to_all | solution.py:137
  50.9 1.9 %fusion.27 = f32[4,4,128,64]{2,3,1,0:T(8,128)} fusion(bf16[6,1,64,128]{3,2,1,0:T(8,128)(2,1)} %collective-permute-done.3, bf16[1,4,64,128]{3,2,1,0:T(8,128)(2,1)} %collective-permute-done.1, bf16[4,4,64,128]{3,2,1,0:T(8,128)(2,1)S(1)} %bitcast.132, bf16[1,4,64,128]{3,2,1,0:T(8,128)(2,1)} %collective-permute-done, bf16[4,4,5,64,64]{4,3,1,0,2:T(8,128)(2,1)S(1)} %reshape.312), kind=kOutput, calls=%fused_computation.53 | convolution fusion | flops 17825792 | bytes 1277952 | tf_op jit(solution)/shard_map/ijab,ijbf->ijaf/dot_general | solution.py:82
  52.8 1.9 %fusion.29 = f32[4,4,128,64]{2,3,1,0:T(8,128)} fusion(bf16[6,1,64,128]{3,2,1,0:T(8,128)(2,1)} %collective-permute-done.2, bf16[1,4,64,128]{3,2,1,0:T(8,128)(2,1)} %collective-permute-done.1, bf16[4,4,64,128]{3,2,1,0:T(8,128)(2,1)S(1)} %bitcast.133, bf16[1,4,64,128]{3,2,1,0:T(8,128)(2,1)} %collective-permute-done, bf16[4,4,5,64,64]{4,3,1,0,2:T(8,128)(2,1)S(1)} %reshape.312), kind=kOutput, calls=%fused_computation.59 | convolution fusion | flops 17825792 | bytes 1277952 | tf_op jit(solution)/shard_map/ijab,ijbf->ijaf/dot_general | solution.py:82
  54.9 4.2 %all-to-all-done.2 = bf16[8,2,64,128]{3,2,1,0:T(8,128)(2,1)S(1)} async-done(((bf16[8,2,64,128]{3,2,1,0:T(8,128)(2,1)}), bf16[8,2,64,128]{3,2,1,0:T(8,128)(2,1)S(1)}, u32[]{:S(2)}, u32[]{:S(2)}) %all-to-all-start.2) | async-done | bytes 262176 | tf_op jit(solution)/shard_map/all_to_all | solution.py:137
  60.5 1.1 %fusion.11 = bf16[4,4,64,128]{3,2,1,0:T(8,128)(2,1)S(1)} fusion(f32[4,4,64,128]{3,2,1,0:T(8,128)S(1)} %bitcast.138, f32[4,4,128,64]{2,3,1,0:T(8,128)S(1)} %copy-done.6, f32[4,4,128,64]{2,3,1,0:T(8,128)S(1)} %copy-done.7, f32[4,4,128,64]{2,3,1,0:T(8,128)S(1)} %convolution_add_fusion.4, bf16[1,4,64,128]{3,2,1,0:T(8,128)(2,1)} %collective-permute-done.1, ...), kind=kOutput, calls=%fused_computation.23 | convolution fusion | flops 17956864 | bytes 2949120 | tf_op jit(solution)/shard_map/ijab,ijbf->ijaf/dot_general | solution.py:82
  62.5 3.7 %collective-permute-start.4 = (bf16[1,4,64,128]{3,2,1,0:T(8,128)(2,1)}, bf16[1,4,64,128]{3,2,1,0:T(8,128)(2,1)}, u32[]{:S(2)}, u32[]{:S(2)}) collective-permute-start(bf16[1,4,64,128]{3,2,1,0:T(8,128)(2,1)} %get-tuple-element.9), channel_id=1, source_target_pairs={{0,4},{4,8},{8,12},{12,16},{16,20},{20,24},{24,28},{1,5},{5,9},{9,... | collective-permute-start | bytes 196616 | tf_op jit(solution)/shard_map/ppermute | solution.py:17
  66.1 1.3 %collective-permute-start.5 = (bf16[1,4,64,128]{3,2,1,0:T(8,128)(2,1)}, bf16[1,4,64,128]{3,2,1,0:T(8,128)(2,1)}, u32[]{:S(2)}, u32[]{:S(2)}) collective-permute-start(bf16[1,4,64,128]{3,2,1,0:T(8,128)(2,1)} %get-tuple-element.10), channel_id=1, source_target_pairs={{4,0},{8,4},{12,8},{16,12},{20,16},{24,20},{28,24},{5,1},{9,5},{13... | collective-permute-start | bytes 196616 | tf_op jit(solution)/shard_map/ppermute | solution.py:18
  70.0 4.3 %all-to-all-start.3 = ((bf16[8,2,64,128]{3,2,1,0:T(8,128)(2,1)}), bf16[8,2,64,128]{3,2,1,0:T(8,128)(2,1)S(1)}, u32[]{:S(2)}, u32[]{:S(2)}) async-start(bf16[8,2,64,128]{3,2,1,0:T(8,128)(2,1)} %copy.95), calls=%async_computation.3 | async-start | bytes 524288 | tf_op jit(solution)/shard_map/all_to_all | solution.py:137
  75.1 5.1 %collective-permute-start.6 = (bf16[6,1,64,128]{3,2,1,0:T(8,128)(2,1)S(1)}, bf16[6,1,64,128]{3,2,1,0:T(8,128)(2,1)S(1)}, u32[]{:S(2)}, u32[]{:S(2)}) collective-permute-start(bf16[6,1,64,128]{3,2,1,0:T(8,128)(2,1)S(1)} %get-tuple-element.5), channel_id=1, source_target_pairs={{0,1},{1,2},{2,3},{4,5},{5,6},{6,7},{8,9},{9,10},{10,11},{12,13},{... | collective-permute-start | bytes 294920 | tf_op jit(solution)/shard_map/ppermute | solution.py:17
  80.2 1.9 %collective-permute-start.7 = (bf16[6,1,64,128]{3,2,1,0:T(8,128)(2,1)S(1)}, bf16[6,1,64,128]{3,2,1,0:T(8,128)(2,1)S(1)}, u32[]{:S(2)}, u32[]{:S(2)}) collective-permute-start(bf16[6,1,64,128]{3,2,1,0:T(8,128)(2,1)S(1)} %get-tuple-element.6), channel_id=1, source_target_pairs={{1,0},{2,1},{3,2},{5,4},{6,5},{7,6},{9,8},{10,9},{11,10},{13,12},{... | collective-permute-start | bytes 294920 | tf_op jit(solution)/shard_map/ppermute | solution.py:18
  82.1 1.1 %convolution_add_fusion.2 = f32[4,4,128,64]{2,3,1,0:T(8,128)S(1)} fusion(f32[4,4,128,64]{2,3,1,0:T(8,128)S(1)} %fusion.40, bf16[4,4,64,128]{3,2,1,0:T(8,128)(2,1)S(1)} %fusion.11, bf16[1,4,64,128]{3,2,1,0:T(8,128)(2,1)} %collective-permute-done.4, bf16[4,4,5,64,64]{4,3,1,0,2:T(8,128)(2,1)S(1)} %reshape.312), kind=kOutput, calls=%fused_computation.14 | convolution fusion | flops 17432576 | bytes 1638400 | tf_op jit(solution)/shard_map/ijab,ijbf->ijaf/dot_general | solution.py:82
  83.2 3.0 %collective-permute-done.7 = bf16[6,1,64,128]{3,2,1,0:T(8,128)(2,1)S(1)} collective-permute-done((bf16[6,1,64,128]{3,2,1,0:T(8,128)(2,1)S(1)}, bf16[6,1,64,128]{3,2,1,0:T(8,128)(2,1)S(1)}, u32[]{:S(2)}, u32[]{:S(2)}) %collective-permute-start.7) | collective-permute-done | bytes 98336 | tf_op jit(solution)/shard_map/ppermute | solution.py:18
  86.4 1.0 %fusion.23 = f32[4,4,128,64]{2,3,1,0:T(8,128)} fusion(bf16[6,1,64,128]{3,2,1,0:T(8,128)(2,1)S(1)} %collective-permute-done.6, bf16[1,4,64,128]{3,2,1,0:T(8,128)(2,1)} %collective-permute-done.5, bf16[4,4,64,128]{3,2,1,0:T(8,128)(2,1)S(1)} %fusion.11, bf16[1,4,64,128]{3,2,1,0:T(8,128)(2,1)} %collective-permute-done.4, ...), kind=kOutput, calls=%fused_computation.44 | convolution fusion | flops 17825792 | bytes 1277952 | tf_op jit(solution)/shard_map/ijab,ijbf->ijaf/dot_general | solution.py:82
  88.7 1.1 %fusion.5 = f32[4,4,64,128]{3,2,1,0:T(8,128)S(1)} fusion(f32[4,4,64,128]{3,2,1,0:T(8,128)S(1)} %bitcast.136, f32[4,4,128,64]{2,3,1,0:T(8,128)S(1)} %fusion.21, f32[4,4,128,64]{2,3,1,0:T(8,128)S(1)} %copy-done.5, f32[4,4,128,64]{2,3,1,0:T(8,128)S(1)} %convolution_add_fusion.2, bf16[1,4,64,128]{3,2,1,0:T(8,128)(2,1)} %collective-permute-done.5, ...), kind=kOutput, calls=%fused_computation.13 | convolution fusion | flops 17825792 | bytes 3211264 | tf_op jit(solution)/shard_map/ijab,ijbf->ijaf/dot_general | solution.py:82
  (106 shorter events, 25.0 us)
Async XLA Ops:
  0.0 23.9 %copy-start = (bf16[1,1,12,4096]{3,2,1,0:T(8,128)(2,1)S(1)}, bf16[1,1,12,4096]{3,2,1,0:T(8,128)(2,1)}, u32[]{:S(2)}) copy-start(bf16[1,1,12,4096]{3,2,1,0:T(8,128)(2,1)} %param.21) | copy-start | bytes 294916
  3.0 27.7 %all-to-all-start = ((bf16[8,1,2]{2,1,0:T(2,128)(2,1)}), bf16[8,1,2]{2,1,0:T(2,128)(2,1)S(1)}, u32[]{:S(2)}, u32[]{:S(2)}) async-start(bf16[8,1,2]{2,1,0:T(2,128)(2,1)} %copy.86), calls=%async_computation | async-start | bytes 8192 | tf_op jit(solution)/shard_map/all_to_all | solution.py:139
  13.1 1.3 %copy-start.3 = (bf16[4,4,64,128]{3,2,1,0:T(8,128)(2,1)S(1)}, bf16[4,4,64,128]{3,2,1,0:T(8,128)(2,1)}, u32[]{:S(2)}) copy-start(bf16[4,4,64,128]{3,2,1,0:T(8,128)(2,1)} %param.12) | copy-start | bytes 786436
  14.8 8.4 %copy-start.14 = (s32[1,1,12]{2,1,0:T(1,128)S(1)}, s32[1,1,12]{2,1,0:T(1,128)}, u32[]{:S(2)}) copy-start(s32[1,1,12]{2,1,0:T(1,128)} %param.18) | copy-start | bytes 148
  14.8 8.4 %copy-start.13 = (f32[32]{0:T(128)S(1)}, f32[32]{0:T(128)}, u32[]{:S(2)}) copy-start(f32[32]{0:T(128)} %param.23) | copy-start | bytes 388
  14.8 10.0 %copy-start.4 = (bf16[4,4,5,4096]{3,1,2,0:T(4,128)(2,1)S(1)}, bf16[4,4,5,4096]{3,1,2,0:T(4,128)(2,1)}, u32[]{:S(2)}) copy-start(bf16[4,4,5,4096]{3,1,2,0:T(4,128)(2,1)} %param.17) | copy-start | bytes 1966084
  15.9 19.7 %collective-permute-start.1 = (bf16[1,4,64,128]{3,2,1,0:T(8,128)(2,1)}, bf16[1,4,64,128]{3,2,1,0:T(8,128)(2,1)}, u32[]{:S(2)}, u32[]{:S(2)}) collective-permute-start(bf16[1,4,64,128]{3,2,1,0:T(8,128)(2,1)} %bitcast.13), channel_id=1, source_target_pairs={{4,0},{8,4},{12,8},{16,12},{20,16},{24,20},{28,24},{5,1},{9,5},{13... | collective-permute-start | bytes 196616 | tf_op jit(solution)/shard_map/ppermute | solution.py:18
  17.9 17.7 %collective-permute-start = (bf16[1,4,64,128]{3,2,1,0:T(8,128)(2,1)}, bf16[1,4,64,128]{3,2,1,0:T(8,128)(2,1)}, u32[]{:S(2)}, u32[]{:S(2)}) collective-permute-start(bf16[1,4,64,128]{3,2,1,0:T(8,128)(2,1)} %bitcast.11), channel_id=1, source_target_pairs={{0,4},{4,8},{8,12},{12,16},{16,20},{20,24},{24,28},{1,5},{5,9},{9,... | collective-permute-start | bytes 196616 | tf_op jit(solution)/shard_map/ppermute | solution.py:17
  30.7 14.5 %all-to-all-start.1 = ((bf16[8,2,4096]{2,1,0:T(2,128)(2,1)}), bf16[8,2,4096]{2,1,0:T(2,128)(2,1)S(1)}, u32[]{:S(2)}, u32[]{:S(2)}) async-start(bf16[8,2,4096]{2,1,0:T(2,128)(2,1)} %copy.88), calls=%async_computation.1 | async-start | bytes 262144 | tf_op jit(solution)/shard_map/all_to_all | solution.py:138
  37.1 15.7 %collective-permute-start.2 = (bf16[6,1,64,128]{3,2,1,0:T(8,128)(2,1)S(1)}, bf16[6,1,64,128]{3,2,1,0:T(8,128)(2,1)}, u32[]{:S(2)}, u32[]{:S(2)}) collective-permute-start(bf16[6,1,64,128]{3,2,1,0:T(8,128)(2,1)S(1)} %get-tuple-element.7), channel_id=1, source_target_pairs={{0,1},{1,2},{2,3},{4,5},{5,6},{6,7},{8,9},{9,10},{10,11},{12,13},{... | collective-permute-start | bytes 294920 | tf_op jit(solution)/shard_map/ppermute | solution.py:17
  42.2 8.7 %collective-permute-start.3 = (bf16[6,1,64,128]{3,2,1,0:T(8,128)(2,1)}, bf16[6,1,64,128]{3,2,1,0:T(8,128)(2,1)}, u32[]{:S(2)}, u32[]{:S(2)}) collective-permute-start(bf16[6,1,64,128]{3,2,1,0:T(8,128)(2,1)} %get-tuple-element.8), channel_id=1, source_target_pairs={{1,0},{2,1},{3,2},{5,4},{6,5},{7,6},{9,8},{10,9},{11,10},{13,12},{... | collective-permute-start | bytes 294920 | tf_op jit(solution)/shard_map/ppermute | solution.py:18
  45.2 13.9 %all-to-all-start.2 = ((bf16[8,2,64,128]{3,2,1,0:T(8,128)(2,1)}), bf16[8,2,64,128]{3,2,1,0:T(8,128)(2,1)S(1)}, u32[]{:S(2)}, u32[]{:S(2)}) async-start(bf16[8,2,64,128]{3,2,1,0:T(8,128)(2,1)} %copy.91), calls=%async_computation.2 | async-start | bytes 524288 | tf_op jit(solution)/shard_map/all_to_all | solution.py:137
  52.8 6.5 %copy-start.10 = (f32[16]{0:T(128)S(1)}, f32[16]{0:T(128)}, u32[]{:S(2)}) copy-start(f32[16]{0:T(128)} %iota_convert_fusion) | copy-start | bytes 196
  59.3 1.2 %copy-start.7 = (f32[4,4,128,64]{2,3,1,0:T(8,128)S(1)}, f32[4,4,128,64]{2,3,1,0:T(8,128)}, u32[]{:S(2)}) copy-start(f32[4,4,128,64]{2,3,1,0:T(8,128)} %fusion.29) | copy-start | bytes 1572868
  61.6 6.4 %copy-start.1 = (f32[1024,128]{1,0:T(8,128)S(1)}, f32[1024,128]{1,0:T(8,128)}, u32[]{:S(2)}) copy-start(f32[1024,128]{1,0:T(8,128)} %fusion.35) | copy-start | bytes 1572868
  61.6 6.4 %copy-start.9 = (bf16[128,128]{1,0:T(8,128)(2,1)S(1)}, bf16[128,128]{1,0:T(8,128)(2,1)}, u32[]{:S(2)}) copy-start(bf16[128,128]{1,0:T(8,128)(2,1)} %convert_element_type.162) | copy-start | bytes 98308
  62.5 11.8 %collective-permute-start.4 = (bf16[1,4,64,128]{3,2,1,0:T(8,128)(2,1)}, bf16[1,4,64,128]{3,2,1,0:T(8,128)(2,1)}, u32[]{:S(2)}, u32[]{:S(2)}) collective-permute-start(bf16[1,4,64,128]{3,2,1,0:T(8,128)(2,1)} %get-tuple-element.9), channel_id=1, source_target_pairs={{0,4},{4,8},{8,12},{12,16},{16,20},{20,24},{24,28},{1,5},{5,9},{9,... | collective-permute-start | bytes 196616 | tf_op jit(solution)/shard_map/ppermute | solution.py:17
  66.1 8.2 %collective-permute-start.5 = (bf16[1,4,64,128]{3,2,1,0:T(8,128)(2,1)}, bf16[1,4,64,128]{3,2,1,0:T(8,128)(2,1)}, u32[]{:S(2)}, u32[]{:S(2)}) collective-permute-start(bf16[1,4,64,128]{3,2,1,0:T(8,128)(2,1)} %get-tuple-element.10), channel_id=1, source_target_pairs={{4,0},{8,4},{12,8},{16,12},{20,16},{24,20},{28,24},{5,1},{9,5},{13... | collective-permute-start | bytes 196616 | tf_op jit(solution)/shard_map/ppermute | solution.py:18
  70.0 17.4 %all-to-all-start.3 = ((bf16[8,2,64,128]{3,2,1,0:T(8,128)(2,1)}), bf16[8,2,64,128]{3,2,1,0:T(8,128)(2,1)S(1)}, u32[]{:S(2)}, u32[]{:S(2)}) async-start(bf16[8,2,64,128]{3,2,1,0:T(8,128)(2,1)} %copy.95), calls=%async_computation.3 | async-start | bytes 524288 | tf_op jit(solution)/shard_map/all_to_all | solution.py:137
  75.1 11.2 %collective-permute-start.6 = (bf16[6,1,64,128]{3,2,1,0:T(8,128)(2,1)S(1)}, bf16[6,1,64,128]{3,2,1,0:T(8,128)(2,1)S(1)}, u32[]{:S(2)}, u32[]{:S(2)}) collective-permute-start(bf16[6,1,64,128]{3,2,1,0:T(8,128)(2,1)S(1)} %get-tuple-element.5), channel_id=1, source_target_pairs={{0,1},{1,2},{2,3},{4,5},{5,6},{6,7},{8,9},{9,10},{10,11},{12,13},{... | collective-permute-start | bytes 294920 | tf_op jit(solution)/shard_map/ppermute | solution.py:17
  80.2 5.9 %collective-permute-start.7 = (bf16[6,1,64,128]{3,2,1,0:T(8,128)(2,1)S(1)}, bf16[6,1,64,128]{3,2,1,0:T(8,128)(2,1)S(1)}, u32[]{:S(2)}, u32[]{:S(2)}) collective-permute-start(bf16[6,1,64,128]{3,2,1,0:T(8,128)(2,1)S(1)} %get-tuple-element.6), channel_id=1, source_target_pairs={{1,0},{2,1},{3,2},{5,4},{6,5},{7,6},{9,8},{10,9},{11,10},{13,12},{... | collective-permute-start | bytes 294920 | tf_op jit(solution)/shard_map/ppermute | solution.py:18
  86.3 1.3 %copy-start.11 = (f32[16]{0:T(128)S(1)}, f32[16]{0:T(128)}, u32[]{:S(2)}) copy-start(f32[16]{0:T(128)} %iota_convert_fusion) | copy-start | bytes 196
  88.7 1.1 %copy-start.8 = (f32[128,128]{1,0:T(8,128)S(1)}, f32[128,128]{1,0:T(8,128)}, u32[]{:S(2)}) copy-start(f32[128,128]{1,0:T(8,128)} %mul.228) | copy-start | bytes 196612
  88.7 1.2 %copy-start.12 = (f32[128]{0:T(128)S(1)}, f32[128]{0:T(128)}, u32[]{:S(2)}) copy-start(f32[128]{0:T(128)} %add.174) | copy-start | bytes 1540
  (3 other events, 3.2 us)
where the time goes:
time: 92.5 us; the launch traced here: 91.2 us
  starting transfers between devices  46 us (50%)
  matrix products  16.2 us (18%)
  local copies, waits for them, and re-layouts  13.2 us (14%)
  other arithmetic  8.1 us (9%)
  waiting for transfers between devices  7.2 us (8%)
    ppermute x4, starting transfers between devices, with_halo(): before = lax.ppermute(last, axis, up)  18.4 us
    all_to_all x2, starting transfers between devices, diffuse(): lax.all_to_all(block_buf, 'rx', split_axis=0, concat_axis=0, tiled=True)  10 us
    dot_general x8, matrix products, block_stencil(): jnp.einsum('ijab,ijbf->ijaf', tiles[:, :, offset], neighbours[offset], pr...  9.27 us
    ppermute x4, starting transfers between devices, with_halo(): after = lax.ppermute(leading, axis, down)  6.4 us
    all_to_all x1, starting transfers between devices, diffuse(): lax.all_to_all(target_buf, 'rx', split_axis=0, concat_axis=0, tiled=True)  6.35 us
    all_to_all x1, starting transfers between devices, diffuse(): lax.all_to_all(tile_buf, 'rx', split_axis=0, concat_axis=0, tiled=True)  4.82 us
    all_to_all x2, waiting for transfers between devices, diffuse(): lax.all_to_all(block_buf, 'rx', split_axis=0, concat_axis=0, tiled=True)  4.22 us
    ppermute x4, waiting for transfers between devices, with_halo(): after = lax.ppermute(leading, axis, down)  2.96 us
  transfers between devices with their start and end apart: 12, of which 2 were waited for; matrix products, arithmetic and copies ran while one was open for 30% of the time, Pallas kernels for 0%

commit v1 on v0

v1 whole, which is shorter than its diff:
```python
import functools

import jax
import jax.numpy as jnp
from jax import lax
from jax.experimental import pallas as pl
from jax.experimental.pallas import tpu as pltpu
from jax.sharding import PartitionSpec as P

DILATION_STEP = 2
CAP = 2
MESH = pl.DeviceIdType.MESH
F32 = jnp.float32
BF16 = jnp.bfloat16


def dot(a, b):
    return jnp.dot(a, b, preferred_element_type=F32)


def each(count, body, limit=8):
    if count <= limit:
        for k in range(count):
            body(k)
    else:

        def step(k, carry):
            body(k)
            return carry

        lax.fori_loop(0, count, step, 0)


def blocks_loop(count, body, unroll):
    def step(k, carry):
        body(k)
        return carry

    lax.fori_loop(0, count, step, 0, unroll=unroll)


def kernel(
    n,
    ny,
    cell,
    w_filter,
    w_gate,
    bias_filter,
    bias_gate,
    adjacency,
    out_block,
    out_dev,
    out_target,
    out_tiles,
    w_mix,
    bias_mix,
    out,
    gated,
    first,
    halo_rows,
    halo_cols,
    send_buf,
    recv_buf,
    target_send,
    target_recv,
    select,
    tiles,
    edge_tiles,
    spread,
    edge_spread,
    table,
    bias_table,
    acc,
    base,
    send_sem,
    recv_sem,
    target_send_sem,
    target_recv_sem,
    halo_send_sem,
    halo_recv_sem,
):
    br, bc, size, feats = cell.shape
    blocks = br * bc
    rows = blocks * size
    half = size // 2
    edges = out_tiles.shape[2]
    channels = w_filter.shape[1]
    steps = feats // channels
    stride = edge_spread.shape[0] // half
    rx = lax.axis_index("rx")
    ry = lax.axis_index("ry")

    barrier = pltpu.get_barrier_semaphore()

    def greet(k):
        pl.semaphore_signal(
            barrier, inc=1, device_id={"rx": lax.rem(rx + k + 1, n)}, device_id_type=MESH
        )

    each(n - 1, greet)

    @pl.when(ry > 0)
    def _():
        pl.semaphore_signal(barrier, inc=1, device_id={"ry": ry - 1}, device_id_type=MESH)

    @pl.when(ry < ny - 1)
    def _():
        pl.semaphore_signal(barrier, inc=1, device_id={"ry": ry + 1}, device_id_type=MESH)

    zero_side = jnp.zeros((2,) + halo_rows.shape[2:], BF16)

    @pl.when(rx == 0)
    def _():
        halo_rows[:, 0] = zero_side

    @pl.when(rx == n - 1)
    def _():
        halo_rows[:, 1] = zero_side

    @pl.when(ry == 0)
    def _():
        halo_cols[:, 0] = zero_side

    @pl.when(ry == ny - 1)
    def _():
        halo_cols[:, 1] = zero_side

    table[...] = jnp.zeros_like(table)
    for t in range(steps):
        span = slice(t * channels, (t + 1) * channels)
        for which, weights in enumerate((w_filter, w_gate)):
            for tap, to in ((1, t), (0, t + DILATION_STEP)):
                if to < steps:
                    at = which * feats + to * channels
                    table[span, at : at + channels] = weights[tap].astype(F32)
        for hop in range(3):
            at = (2 + hop) * feats + t * channels
            table[span, at : at + channels] = w_mix[hop].astype(F32)
        bias_table[0:1, span] = bias_filter[...]
        bias_table[1:2, span] = bias_gate[...]
        bias_table[2:3, span] = bias_mix[...]
    taps = table[:, : 2 * feats].astype(BF16)
    mixes = [table[:, (2 + h) * feats : (3 + h) * feats].astype(BF16) for h in range(3)]

    for i in range(br):
        pre = dot(cell[i].reshape(bc * size, feats), taps)
        pre_f = pre[:, :feats] + bias_table[0:1]
        pre_g = pre[:, feats:] + bias_table[1:2]
        value = jnp.tanh(pre_f) * (0.5 * jnp.tanh(0.5 * pre_g) + 0.5)
        gated[i] = value.astype(BF16).reshape(bc, size, feats)

    for r in range(half):
        piece = out_tiles[0, 0, :, r * 2 * size : (r + 1) * 2 * size]
        edge_spread[r * stride : r * stride + edges] = piece.astype(F32)
    for e in range(edges):
        pairs = edge_spread[pl.ds(e, half, stride=stride), :]
        edge_tiles[e, :half] = pairs.astype(BF16)
        edge_tiles[e, half:] = pltpu.roll(pairs, size, 1).astype(BF16)

    def slots(d):
        head, tail = jnp.int32(-1), jnp.int32(-1)
        for e in range(edges):
            hit = out_dev[0, 0, e, 0] == d
            head = jnp.where(hit & (head < 0), e, head)
            tail = jnp.where(hit, e, tail)
        return ((jnp.maximum(head, 0), head >= 0), (jnp.maximum(tail, 0), tail != head))

    lane = lax.broadcasted_iota(jnp.int32, (8, CAP * size), 1)

    def halo_copies(signal, hop):
        sides = []
        for which, (axis, here, count, halo) in enumerate(
            (("rx", rx, n, halo_rows), ("ry", ry, ny, halo_cols))
        ):
            last = (br if which == 0 else bc) - 1
            for side, (edge, step) in enumerate(((last, 1), (0, -1))):
                src = signal.at[edge] if which == 0 else signal.at[:, edge]
                copy = pltpu.make_async_remote_copy(
                    src_ref=src,
                    dst_ref=halo.at[hop, side],
                    send_sem=halo_send_sem.at[hop, which, side],
                    recv_sem=halo_recv_sem.at[hop, which, side],
                    device_id={axis: jnp.clip(here + step, 0, count - 1)},
                    device_id_type=MESH,
                )
                sends = (here < count - 1) if step == 1 else (here > 0)
                gets = (here > 0) if step == 1 else (here < count - 1)
                sides.append((sends, gets, copy))
        return sides

    def far_copy(hop, d, source):
        return pltpu.make_async_remote_copy(
            src_ref=send_buf.at[hop, d],
            dst_ref=recv_buf.at[hop, source],
            send_sem=send_sem.at[hop, d],
            recv_sem=recv_sem.at[hop, source],
            device_id={"rx": d},
            device_id_type=MESH,
        )

    def target_copy(d, source):
        return pltpu.make_async_remote_copy(
            src_ref=target_send.at[d],
            dst_ref=target_recv.at[source],
            send_sem=target_send_sem.at[d],
            recv_sem=target_recv_sem.at[source],
            device_id={"rx": d},
            device_id_type=MESH,
        )

    def send_far(signal, hop):
        def one(k):
            d = lax.rem(rx + k + 1, n)
            products, targets = [], []
            for index, valid in slots(d):
                b = out_block[0, 0, index]
                block = signal[lax.div(b, bc), lax.rem(b, bc)]
                product = dot(edge_tiles[index][:, :size], block)
                products.append((product * jnp.where(valid, 1.0, 0.0)).astype(BF16))
                targets.append(jnp.where(valid, out_target[0, 0, index], -1))
            both = jnp.concatenate(products, axis=0)
            named = jnp.where(lane < size, targets[0], targets[1]).astype(F32)
            own = k == n - 1

            def keep():
                recv_buf[hop, rx] = both
                if hop == 0:
                    target_recv[rx] = named

            def send():
                send_buf[hop, d] = both
                far_copy(hop, d, rx).start()
                if hop == 0:
                    target_send[d] = named
                    target_copy(d, rx).start()

            if isinstance(own, bool):
                keep() if own else send()
            else:
                pl.when(own)(keep)
                pl.when(jnp.logical_not(own))(send)

        each(n, one)

    def wait_far(hop):
        def one(k):
            source = lax.rem(rx + n - k - 1, n)
            far_copy(hop, source, source).wait_recv()

        each(n - 1, one)

    def near(signal, hop):
        for i in range(br):
            for j in range(bc):
                up = signal[i - 1, j] if i > 0 else halo_rows[hop, 0, j]
                down = signal[i + 1, j] if i < br - 1 else halo_rows[hop, 1, j]
                left = signal[i, j - 1] if j > 0 else halo_cols[hop, 0, i]
                right = signal[i, j + 1] if j < bc - 1 else halo_cols[hop, 1, i]
                column = jnp.concatenate([signal[i, j], up, down, left, right], axis=0)
                total = dot(tiles[i * bc + j][:, : 5 * size], column)
                at = (i * bc + j) * size
                acc[pl.ds(at, half, stride=2), :] = total[:half]
                acc[pl.ds(at + 1, half, stride=2), :] = total[half:]

    pl.semaphore_wait(
        barrier,
        n - 1 + jnp.where(ry > 0, 1, 0) + jnp.where(ry < ny - 1, 1, 0),
    )

    def start_hop(signal, hop):
        for sends, gets, copy in halo_copies(signal, hop):
            pl.when(sends)(copy.start)
        send_far(signal, hop)

    def wait_halo(signal, hop):
        for sends, gets, copy in halo_copies(signal, hop):
            pl.when(gets)(copy.wait_recv)

    start_hop(gated, 0)

    low = lax.broadcasted_iota(jnp.int32, (half, 2 * size), 1) < size

    def arrange(ij):
        slot = lax.rem(ij, spread.shape[0])
        i, j = lax.div(ij, bc), lax.rem(ij, bc)
        for r in range(half):
            piece = adjacency[i, j, :, r * 2 * size : (r + 1) * 2 * size]
            spread[slot, r * 8 : r * 8 + 5] = piece.astype(F32)
        pairs = [spread[slot, pl.ds(k, half, stride=8), :] for k in range(5)]
        turned = [pltpu.roll(pair, size, 1) for pair in pairs]
        zero = jnp.zeros_like(pairs[0])
        pairs.append(zero)
        turned.append(zero)
        for k in range(0, 6, 2):
            span = slice(k * size, (k + 2) * size)
            tiles[ij, :half, span] = jnp.where(low, pairs[k], turned[k + 1]).astype(BF16)
            tiles[ij, half:, span] = jnp.where(low, turned[k], pairs[k + 1]).astype(BF16)

    blocks_loop(blocks, arrange, 4)

    wait_halo(gated, 0)
    near(gated, 0)

    def wait_target(k):
        source = lax.rem(rx + n - k - 1, n)
        target_copy(source, source).wait_recv()

    each(n - 1, wait_target)
    spot = lax.broadcasted_iota(jnp.int32, (size, CAP * size), 1) % size
    row = lax.broadcasted_iota(jnp.int32, (size, CAP * size), 0)
    unit = jnp.where(row == 2 * (spot % half) + spot // half, 1.0, 0.0).astype(BF16)
    for source in range(n):
        named = target_recv[source, 0:1]
        span = slice(source * CAP * size, (source + 1) * CAP * size)
        for block in range(blocks):
            hit = jnp.where(named == float(block), 1.0, 0.0).astype(BF16)
            select[block * size : (block + 1) * size, span] = unit * hit

    wait_far(0)
    landed = recv_buf[0].reshape(n * CAP * size, feats)
    strip = bc * size
    for i in range(br):
        total = acc[i * strip : (i + 1) * strip] + dot(select[i * strip : (i + 1) * strip], landed)
        first[i] = total.astype(BF16).reshape(bc, size, feats)

    start_hop(first, 1)

    for i in range(br):
        own = dot(gated[i].reshape(strip, feats), mixes[0])
        own = own + dot(first[i].reshape(strip, feats), mixes[1]) + bias_table[2:3]
        base[i * strip : (i + 1) * strip] = own + cell[i].reshape(strip, feats).astype(F32)
    wait_halo(first, 1)
    near(first, 1)

    wait_far(1)
    landed = recv_buf[1].reshape(n * CAP * size, feats)
    for i in range(br):
        span = slice(i * strip, (i + 1) * strip)
        second = acc[span] + dot(select[span], landed)
        upper = second.astype(BF16)
        lower = (second - upper.astype(F32)).astype(BF16)
        total = base[span] + (dot(upper, mixes[2]) + dot(lower, mixes[2]))
        out[i] = total.astype(BF16).reshape(bc, size, feats)

    for hop, signal in enumerate((gated, first)):
        for sends, gets, copy in halo_copies(signal, hop):
            pl.when(sends)(copy.wait_send)

        def sent(k):
            d = lax.rem(rx + k + 1, n)
            far_copy(hop, d, rx).wait_send()
            if hop == 0:
                target_copy(d, rx).wait_send()

        each(n - 1, sent)


def local(
    n,
    ny,
    cell_input,
    w_filter,
    w_gate,
    bias_filter,
    bias_gate,
    adjacency,
    out_block,
    out_dev,
    out_target,
    out_tiles,
    w_mix,
    bias_mix,
):
    br, bc, size, feats = cell_input.shape
    blocks = br * bc
    rows = blocks * size
    edges = out_tiles.shape[2]
    channels = w_filter.shape[1]
    half = size // 2
    stride = -(-edges // 8) * 8
    assert feats == 128 and size == 64 and br == bc
    vmem = pl.BlockSpec(memory_space=pltpu.VMEM)
    smem = pl.BlockSpec(memory_space=pltpu.SMEM)
    dma = pltpu.SemaphoreType.DMA
    scratch = [
        pltpu.VMEM((br, bc, size, feats), BF16),
        pltpu.VMEM((br, bc, size, feats), BF16),
        pltpu.VMEM((2, 2, bc, size, feats), BF16),
        pltpu.VMEM((2, 2, br, size, feats), BF16),
        pltpu.VMEM((2, n, CAP * size, feats), BF16),
        pltpu.VMEM((2, n, CAP * size, feats), BF16),
        pltpu.VMEM((n, 8, CAP * size), F32),
        pltpu.VMEM((n, 8, CAP * size), F32),
        pltpu.VMEM((rows, n * CAP * size), BF16),
        pltpu.VMEM((blocks, size, 6 * size), BF16),
        pltpu.VMEM((edges, size, 2 * size), BF16),
        pltpu.VMEM((4, half * 8, 2 * size), F32),
        pltpu.VMEM((half * stride, 2 * size), F32),
        pltpu.VMEM((feats, 5 * feats), F32),
        pltpu.VMEM((8, feats), F32),
        pltpu.VMEM((rows, feats), F32),
        pltpu.VMEM((rows, feats), F32),
        dma((2, n)),
        dma((2, n)),
        dma((n,)),
        dma((n,)),
        dma((2, 2, 2)),
        dma((2, 2, 2)),
    ]
    near_flops = 2 * 2 * 5 * rows * size * feats
    return pl.pallas_call(
        functools.partial(kernel, n, ny),
        out_shape=jax.ShapeDtypeStruct(cell_input.shape, BF16),
        in_specs=[vmem] * 6 + [smem] * 3 + [vmem] * 3,
        out_specs=vmem,
        scratch_shapes=scratch,
        cost_estimate=pl.CostEstimate(
            flops=near_flops, bytes_accessed=2 * rows * feats * 2, transcendentals=2 * rows * feats
        ),
        compiler_params=pltpu.CompilerParams(
            collective_id=0, has_side_effects=True, vmem_limit_bytes=40 * 1024 * 1024
        ),
    )(
        cell_input,
        w_filter,
        w_gate,
        bias_filter.reshape(1, channels),
        bias_gate.reshape(1, channels),
        adjacency,
        out_block,
        out_dev,
        out_target,
        out_tiles,
        w_mix,
        bias_mix.reshape(1, channels),
    )


def solution(mesh):
    in_specs = (
        P("rx", "ry", None, None),
        P(),
        P(),
        P(),
        P(),
        P("rx", "ry", None, None),
        P("rx", "ry", None),
        P("rx", "ry", None, None),
        P("rx", "ry", None),
        P("rx", "ry", None, None),
        P(),
        P(),
    )
    out_specs = P("rx", "ry", None, None)
    body = functools.partial(local, mesh.shape["rx"], mesh.shape["ry"])
    return jax.shard_map(body, mesh=mesh, in_specs=in_specs, out_specs=out_specs, check_vma=False)
```

time: 92.5 us -> 27.8 us (0.30)
  the two profiles are of different devices: /device:TPU:1 before, /device:TPU:0 now
where the time goes in v1:
time: 27.8 us; the launch traced here: 27.7 us
  Pallas kernels  24.5 us (88%)
  local copies, waits for them, and re-layouts  3.07 us (11%)
    pallas_call x1, Pallas kernels, local(): pl.pallas_call(functools.partial(kernel, n, ny), out_shape=jax.ShapeDtype...  24.5 us
    unnamed x25, local copies, waits for them, and re-layouts  3.07 us

profile of v1, /device:TPU:0, one launch (start us, length us, event | category | flops | bytes accessed | tf_op | source)
XLA Modules:
  0.0 27.7 jit_solution(9910400050682809319)
XLA Ops:
  0.0 0.0 copy-start.10
  0.0 0.7 %copy-done.10 = s32[1,1,12,1]{2,3,1,0:T(1,128)S(1)} copy-done((s32[1,1,12,1]{2,3,1,0:T(1,128)S(1)}, s32[1,1,12,1]{2,3,1,0:T(1,128)}, u32[]{:S(2)}) %copy-start.10) | copy-done | bytes 72
  0.7 0.1 copy.14.out_dev
  0.8 0.0 copy-start
  0.8 0.0 copy-start.1
  0.8 0.0 copy-start.4
  0.8 0.0 copy-start.5
  0.8 0.0 copy-start.6
  0.8 0.0 copy-start.7
  0.8 0.0 copy-start.8
  0.8 0.0 copy-start.9
  0.8 1.6 %copy.13.adjacency = bf16[4,4,5,4096]{3,2,1,0:T(8,128)(2,1)S(1)} copy(bf16[4,4,5,4096]{3,1,2,0:T(4,128)(2,1)} %param.17) | data formatting | bytes 1310720 | tf_op args[5]
  2.4 0.0 copy-done
  2.4 0.0 copy-done.1
  2.4 0.0 copy-done.2
  2.4 0.0 copy-done.3
  2.4 0.0 copy-done.4
  2.5 0.0 copy-done.5
  2.5 0.0 copy-done.6
  2.5 0.0 copy-done.7
  2.5 0.0 copy-done.8
  2.5 0.0 copy-done.9
  2.5 24.5 %shard_map.118 = bf16[4,4,64,128]{3,2,1,0:T(8,128)(2,1)S(1)} custom-call(bf16[4,4,64,128]{3,2,1,0:T(8,128)(2,1)S(1)} %copy-done, bf16[2,32,32]{2,1,0:T(8,128)(2,1)S(1)} %copy-done.3, bf16[2,32,32]{2,1,0:T(8,128)(2,1)S(1)} %copy-done.4, f32[1,32]{1,0:T(1,128)S(1)} %bitcast.3, f32[1,32]{1,0:T(1,128)S(1)} %bitcast.4, ...), custom_call_target="tpu_custom_call" | custom-call | flops 167772160 | bytes 524288 | tf_op jit(solution)/shard_map/pallas_call | solution.py:411
  27.0 0.7 %copy.16 = bf16[4,4,64,128]{3,2,1,0:T(8,128)(2,1)} copy(bf16[4,4,64,128]{3,2,1,0:T(8,128)(2,1)S(1)} %shard_map.118) | data formatting | bytes 524288
  (2 shorter events, 0.0 us)
Async XLA Ops:
  0.0 0.7 %copy-start.10 = (s32[1,1,12,1]{2,3,1,0:T(1,128)S(1)}, s32[1,1,12,1]{2,3,1,0:T(1,128)}, u32[]{:S(2)}) copy-start(s32[1,1,12,1]{2,3,1,0:T(1,128)} %param.19) | copy-start | bytes 148
  0.8 1.7 %copy-start = (bf16[4,4,64,128]{3,2,1,0:T(8,128)(2,1)S(1)}, bf16[4,4,64,128]{3,2,1,0:T(8,128)(2,1)}, u32[]{:S(2)}) copy-start(bf16[4,4,64,128]{3,2,1,0:T(8,128)(2,1)} %cell.1) | copy-start | bytes 786436
  0.8 1.7 %copy-start.1 = (bf16[1,1,12,4096]{3,2,1,0:T(8,128)(2,1)S(1)}, bf16[1,1,12,4096]{3,2,1,0:T(8,128)(2,1)}, u32[]{:S(2)}) copy-start(bf16[1,1,12,4096]{3,2,1,0:T(8,128)(2,1)} %out_tiles.1) | copy-start | bytes 294916
  0.8 1.7 %copy-start.2 = (bf16[3,32,32]{2,1,0:T(8,128)(2,1)S(1)}, bf16[3,32,32]{2,1,0:T(8,128)(2,1)}, u32[]{:S(2)}) copy-start(bf16[3,32,32]{2,1,0:T(8,128)(2,1)} %w_mix.1) | copy-start | bytes 18436
  0.8 1.7 %copy-start.3 = (bf16[2,32,32]{2,1,0:T(8,128)(2,1)S(1)}, bf16[2,32,32]{2,1,0:T(8,128)(2,1)}, u32[]{:S(2)}) copy-start(bf16[2,32,32]{2,1,0:T(8,128)(2,1)} %w_filter.1) | copy-start | bytes 12292
  0.8 1.7 %copy-start.4 = (bf16[2,32,32]{2,1,0:T(8,128)(2,1)S(1)}, bf16[2,32,32]{2,1,0:T(8,128)(2,1)}, u32[]{:S(2)}) copy-start(bf16[2,32,32]{2,1,0:T(8,128)(2,1)} %w_gate.1) | copy-start | bytes 12292
  0.8 1.7 %copy-start.5 = (f32[32]{0:T(128)S(1)}, f32[32]{0:T(128)}, u32[]{:S(2)}) copy-start(f32[32]{0:T(128)} %param.15) | copy-start | bytes 388
  0.8 1.7 %copy-start.6 = (f32[32]{0:T(128)S(1)}, f32[32]{0:T(128)}, u32[]{:S(2)}) copy-start(f32[32]{0:T(128)} %param.16) | copy-start | bytes 388
  0.8 1.7 %copy-start.7 = (s32[1,1,12]{2,1,0:T(1,128)S(1)}, s32[1,1,12]{2,1,0:T(1,128)}, u32[]{:S(2)}) copy-start(s32[1,1,12]{2,1,0:T(1,128)} %out_block.1) | copy-start | bytes 148
  0.8 1.7 %copy-start.8 = (s32[1,1,12]{2,1,0:T(1,128)S(1)}, s32[1,1,12]{2,1,0:T(1,128)}, u32[]{:S(2)}) copy-start(s32[1,1,12]{2,1,0:T(1,128)} %out_target.1) | copy-start | bytes 148
  0.8 1.7 %copy-start.9 = (f32[32]{0:T(128)S(1)}, f32[32]{0:T(128)}, u32[]{:S(2)}) copy-start(f32[32]{0:T(128)} %param.23) | copy-start | bytes 388

commit v2 on v1

--- a/solution.py
+++ b/solution.py
@@ -42,19 +42,24 @@
 def kernel(
     n,
     ny,
-    cell,
-    w_filter,
-    w_gate,
-    bias_filter,
-    bias_gate,
-    adjacency,
-    out_block,
-    out_dev,
-    out_target,
-    out_tiles,
-    w_mix,
-    bias_mix,
-    out,
+    *refs,
+):
+    inputs, (out, *landing), refs = refs[:12], refs[12:25], refs[25:]
+    (
+        cell,
+        w_filter,
+        w_gate,
+        bias_filter,
+        bias_gate,
+        adjacency,
+        out_block,
+        out_dev,
+        out_target,
+        out_tiles,
+        w_mix,
+        bias_mix,
+    ) = landing
+    (
     gated,
     first,
     halo_rows,
@@ -78,7 +83,14 @@
     target_recv_sem,
     halo_send_sem,
     halo_recv_sem,
-):
+    fetch_sem,
+    ) = refs
+    fetches = [
+        pltpu.make_async_copy(src, dst, fetch_sem.at[k])
+        for k, (src, dst) in enumerate(zip(inputs, landing))
+    ]
+    for k in (1, 2, 3, 4, 9, 6, 7, 8, 0, 10, 11, 5):
+        fetches[k].start()
     br, bc, size, feats = cell.shape
     blocks = br * bc
     rows = blocks * size
@@ -124,6 +136,10 @@
     @pl.when(ry == ny - 1)
     def _():
         halo_cols[:, 1] = zero_side
+
+    for k in range(12):
+        if k != 5:
+            fetches[k].wait()
 
     table[...] = jnp.zeros_like(table)
     for t in range(steps):
@@ -142,12 +158,12 @@
     taps = table[:, : 2 * feats].astype(BF16)
     mixes = [table[:, (2 + h) * feats : (3 + h) * feats].astype(BF16) for h in range(3)]
 
-    for i in range(br):
-        pre = dot(cell[i].reshape(bc * size, feats), taps)
+    def gate(block_rows):
+        pre = dot(block_rows, taps)
         pre_f = pre[:, :feats] + bias_table[0:1]
         pre_g = pre[:, feats:] + bias_table[1:2]
         value = jnp.tanh(pre_f) * (0.5 * jnp.tanh(0.5 * pre_g) + 0.5)
-        gated[i] = value.astype(BF16).reshape(bc, size, feats)
+        return value.astype(BF16)
 
     for r in range(half):
         piece = out_tiles[0, 0, :, r * 2 * size : (r + 1) * 2 * size]
@@ -160,7 +176,7 @@
     def slots(d):
         head, tail = jnp.int32(-1), jnp.int32(-1)
         for e in range(edges):
-            hit = out_dev[0, 0, e, 0] == d
+            hit = out_dev[0, 0, e] == d
             head = jnp.where(hit & (head < 0), e, head)
             tail = jnp.where(hit, e, tail)
         return ((jnp.maximum(head, 0), head >= 0), (jnp.maximum(tail, 0), tail != head))
@@ -208,16 +224,30 @@
             device_id_type=MESH,
         )
 
+    part = n // 2
+
+    def destination(k):
+        side = (rx // part + 1 + k // part) % 2
+        return side * part + (rx % part + k % part + 1) % part
+
     def send_far(signal, hop):
         def one(k):
-            d = lax.rem(rx + k + 1, n)
-            products, targets = [], []
+            d = destination(k)
+            picked, targets = [], []
             for index, valid in slots(d):
                 b = out_block[0, 0, index]
                 block = signal[lax.div(b, bc), lax.rem(b, bc)]
+                picked.append((index, valid, block))
+                targets.append(jnp.where(valid, out_target[0, 0, index], -1))
+            if hop == 0:
+                both = gate(jnp.concatenate([block for _, _, block in picked], axis=0))
+                values = [both[c * size : (c + 1) * size] for c in range(CAP)]
+            else:
+                values = [block for _, _, block in picked]
+            products = []
+            for (index, valid, _), block in zip(picked, values):
                 product = dot(edge_tiles[index][:, :size], block)
                 products.append((product * jnp.where(valid, 1.0, 0.0)).astype(BF16))
-                targets.append(jnp.where(valid, out_target[0, 0, index], -1))
             both = jnp.concatenate(products, axis=0)
             named = jnp.where(lane < size, targets[0], targets[1]).astype(F32)
             own = k == n - 1
@@ -242,12 +272,34 @@
 
         each(n, one)
 
-    def wait_far(hop):
-        def one(k):
-            source = lax.rem(rx + n - k - 1, n)
+    part_pairs = n // 4
+
+    def add_far(hop, finish):
+        strip = bc * size
+
+        def wait_source(source):
             far_copy(hop, source, source).wait_recv()
 
-        each(n - 1, one)
+        def one(q):
+            side = (rx // part + q // part_pairs) % 2
+            pair = side * part_pairs + (rx % part // 2 + q % part_pairs) % part_pairs
+            if isinstance(q, int) and q == 0:
+                wait_source(rx + 1 - 2 * (rx % 2))
+            else:
+                wait_source(2 * pair)
+                wait_source(2 * pair + 1)
+            landed = recv_buf[hop, pl.ds(2 * pair, 2)].reshape(2 * CAP * size, feats)
+            for i in range(br):
+                span = slice(i * strip, (i + 1) * strip)
+                total = acc[span] + dot(select[pair, span], landed)
+                if isinstance(q, int) and q == n // 2 - 1:
+                    finish(i, total)
+                else:
+                    acc[span] = total
+
+        one(0)
+        each(n // 2 - 2, lambda q: one(q + 1))
+        one(n // 2 - 1)
 
     def near(signal, hop):
         for i in range(br):
@@ -267,36 +319,45 @@
         n - 1 + jnp.where(ry > 0, 1, 0) + jnp.where(ry < ny - 1, 1, 0),
     )
 
-    def start_hop(signal, hop):
+    def start_halo(signal, hop):
         for sends, gets, copy in halo_copies(signal, hop):
             pl.when(sends)(copy.start)
-        send_far(signal, hop)
 
     def wait_halo(signal, hop):
         for sends, gets, copy in halo_copies(signal, hop):
             pl.when(gets)(copy.wait_recv)
 
-    start_hop(gated, 0)
+    send_far(cell, 0)
+    for i in range(br):
+        gated[i] = gate(cell[i].reshape(bc * size, feats)).reshape(bc, size, feats)
+    start_halo(gated, 0)
 
     low = lax.broadcasted_iota(jnp.int32, (half, 2 * size), 1) < size
 
-    def arrange(ij):
-        slot = lax.rem(ij, spread.shape[0])
-        i, j = lax.div(ij, bc), lax.rem(ij, bc)
-        for r in range(half):
-            piece = adjacency[i, j, :, r * 2 * size : (r + 1) * 2 * size]
-            spread[slot, r * 8 : r * 8 + 5] = piece.astype(F32)
-        pairs = [spread[slot, pl.ds(k, half, stride=8), :] for k in range(5)]
-        turned = [pltpu.roll(pair, size, 1) for pair in pairs]
-        zero = jnp.zeros_like(pairs[0])
-        pairs.append(zero)
-        turned.append(zero)
-        for k in range(0, 6, 2):
-            span = slice(k * size, (k + 2) * size)
-            tiles[ij, :half, span] = jnp.where(low, pairs[k], turned[k + 1]).astype(BF16)
-            tiles[ij, half:, span] = jnp.where(low, turned[k], pairs[k + 1]).astype(BF16)
-
-    blocks_loop(blocks, arrange, 4)
+    def arrange(i):
+        slot = lax.rem(i, spread.shape[0])
+        for k in range(5):
+            for r in range(half):
+                piece = adjacency[i, k, :, r * 2 * size : (r + 1) * 2 * size]
+                at = r * 8 + k % 2 * bc
+                spread[slot, k // 2, at : at + bc] = piece.astype(F32)
+        for j in range(bc):
+            pairs = [
+                spread[slot, k // 2, pl.ds(k % 2 * bc + j, half, stride=8), :] for k in range(5)
+            ]
+            turned = [pltpu.roll(pair, size, 1) for pair in pairs]
+            zero = jnp.zeros_like(pairs[0])
+            pairs.append(zero)
+            turned.append(zero)
+            for k in range(0, 6, 2):
+                span = slice(k * size, (k + 2) * size)
+                even = jnp.where(low, pairs[k], turned[k + 1])
+                odd = jnp.where(low, turned[k], pairs[k + 1])
+                tiles[i * bc + j, :half, span] = even.astype(BF16)
+                tiles[i * bc + j, half:, span] = odd.astype(BF16)
+
+    fetches[5].wait()
+    blocks_loop(br, arrange, 2)
 
     wait_halo(gated, 0)
     near(gated, 0)
@@ -311,19 +372,19 @@
     unit = jnp.where(row == 2 * (spot % half) + spot // half, 1.0, 0.0).astype(BF16)
     for source in range(n):
         named = target_recv[source, 0:1]
-        span = slice(source * CAP * size, (source + 1) * CAP * size)
+        span = slice(source % 2 * CAP * size, (source % 2 + 1) * CAP * size)
         for block in range(blocks):
             hit = jnp.where(named == float(block), 1.0, 0.0).astype(BF16)
-            select[block * size : (block + 1) * size, span] = unit * hit
-
-    wait_far(0)
-    landed = recv_buf[0].reshape(n * CAP * size, feats)
+            select[source // 2, block * size : (block + 1) * size, span] = unit * hit
+
     strip = bc * size
-    for i in range(br):
-        total = acc[i * strip : (i + 1) * strip] + dot(select[i * strip : (i + 1) * strip], landed)
+
+    def end_first(i, total):
         first[i] = total.astype(BF16).reshape(bc, size, feats)
 
-    start_hop(first, 1)
+    add_far(0, end_first)
+    send_far(first, 1)
+    start_halo(first, 1)
 
     for i in range(br):
         own = dot(gated[i].reshape(strip, feats), mixes[0])
@@ -332,22 +393,21 @@
     wait_halo(first, 1)
     near(first, 1)
 
-    wait_far(1)
-    landed = recv_buf[1].reshape(n * CAP * size, feats)
-    for i in range(br):
-        span = slice(i * strip, (i + 1) * strip)
-        second = acc[span] + dot(select[span], landed)
+    def end_second(i, second):
         upper = second.astype(BF16)
         lower = (second - upper.astype(F32)).astype(BF16)
-        total = base[span] + (dot(upper, mixes[2]) + dot(lower, mixes[2]))
+        total = base[i * strip : (i + 1) * strip]
+        total = total + (dot(upper, mixes[2]) + dot(lower, mixes[2]))
         out[i] = total.astype(BF16).reshape(bc, size, feats)
+
+    add_far(1, end_second)
 
     for hop, signal in enumerate((gated, first)):
         for sends, gets, copy in halo_copies(signal, hop):
             pl.when(sends)(copy.wait_send)
 
         def sent(k):
-            d = lax.rem(rx + k + 1, n)
+            d = destination(k)
             far_copy(hop, d, rx).wait_send()
             if hop == 0:
                 target_copy(d, rx).wait_send()
@@ -378,11 +438,28 @@
     channels = w_filter.shape[1]
     half = size // 2
     stride = -(-edges // 8) * 8
-    assert feats == 128 and size == 64 and br == bc
+    assert feats == 128 and size == 64 and br == bc == 4 and n % 4 == 0
     vmem = pl.BlockSpec(memory_space=pltpu.VMEM)
-    smem = pl.BlockSpec(memory_space=pltpu.SMEM)
     dma = pltpu.SemaphoreType.DMA
+    hbm = pl.BlockSpec(memory_space=pltpu.HBM)
+    operands = (
+        cell_input,
+        w_filter,
+        w_gate,
+        bias_filter.reshape(1, channels),
+        bias_gate.reshape(1, channels),
+        adjacency.transpose(0, 2, 1, 3),
+        out_block,
+        out_dev.reshape(out_block.shape),
+        out_target,
+        out_tiles,
+        w_mix,
+        bias_mix.reshape(1, channels),
+    )
     scratch = [
+        (pltpu.SMEM if k in (6, 7, 8) else pltpu.VMEM)(a.shape, a.dtype)
+        for k, a in enumerate(operands)
+    ] + [
         pltpu.VMEM((br, bc, size, feats), BF16),
         pltpu.VMEM((br, bc, size, feats), BF16),
         pltpu.VMEM((2, 2, bc, size, feats), BF16),
@@ -391,10 +468,10 @@
         pltpu.VMEM((2, n, CAP * size, feats), BF16),
         pltpu.VMEM((n, 8, CAP * size), F32),
         pltpu.VMEM((n, 8, CAP * size), F32),
-        pltpu.VMEM((rows, n * CAP * size), BF16),
+        pltpu.VMEM((n // 2, rows, 2 * CAP * size), BF16),
         pltpu.VMEM((blocks, size, 6 * size), BF16),
         pltpu.VMEM((edges, size, 2 * size), BF16),
-        pltpu.VMEM((4, half * 8, 2 * size), F32),
+        pltpu.VMEM((2, 3, half * 8, 2 * size), F32),
         pltpu.VMEM((half * stride, 2 * size), F32),
         pltpu.VMEM((feats, 5 * feats), F32),
         pltpu.VMEM((8, feats), F32),
@@ -406,34 +483,22 @@
         dma((n,)),
         dma((2, 2, 2)),
         dma((2, 2, 2)),
+        dma((12,)),
     ]
     near_flops = 2 * 2 * 5 * rows * size * feats
     return pl.pallas_call(
         functools.partial(kernel, n, ny),
         out_shape=jax.ShapeDtypeStruct(cell_input.shape, BF16),
-        in_specs=[vmem] * 6 + [smem] * 3 + [vmem] * 3,
+        in_specs=[hbm] * 12,
         out_specs=vmem,
         scratch_shapes=scratch,
         cost_estimate=pl.CostEstimate(
             flops=near_flops, bytes_accessed=2 * rows * feats * 2, transcendentals=2 * rows * feats
         ),
         compiler_params=pltpu.CompilerParams(
-            collective_id=0, has_side_effects=True, vmem_limit_bytes=40 * 1024 * 1024
+            collective_id=0, has_side_effects=True, vmem_limit_bytes=63 * 1024 * 1024
         ),
-    )(
-        cell_input,
-        w_filter,
-        w_gate,
-        bias_filter.reshape(1, channels),
-        bias_gate.reshape(1, channels),
-        adjacency,
-        out_block,
-        out_dev,
-        out_target,
-        out_tiles,
-        w_mix,
-        bias_mix.reshape(1, channels),
-    )
+    )(*operands)
 
 
 def solution(mesh):

time: 27.8 us -> 28.9 us (1.040); the launches traced: 27.7 us -> 28.5 us
  Pallas kernels: 24.5 us -> 26.8 us
  local copies, waits for them, and re-layouts: 3.07 us -> 1.67 us
    pallas_call x1, Pallas kernels: 24.5 us -> 26.8 us  [local(): pl.pallas_call(functools.partial(kernel, n, ny), out_shape=jax.ShapeDtype...]
    unnamed x25 -> x1, local copies, waits for them, and re-layouts: 3.07 us -> 1.67 us
where the time goes in v2:
time: 28.9 us; the launch traced here: 28.5 us
  Pallas kernels  26.8 us (93%)
  local copies, waits for them, and re-layouts  1.67 us (6%)
    pallas_call x1, Pallas kernels, local(): pl.pallas_call(functools.partial(kernel, n, ny), out_shape=jax.ShapeDtype...  26.8 us
    unnamed x1, local copies, waits for them, and re-layouts  1.67 us

profile of v2, /device:TPU:0, one launch (start us, length us, event | category | flops | bytes accessed | tf_op | source)
XLA Modules:
  0.0 28.5 jit_solution(12919958614933704808)
XLA Ops:
  0.0 26.8 %shard_map.118 = bf16[4,4,64,128]{3,2,1,0:T(8,128)(2,1)} custom-call(bf16[4,4,64,128]{3,2,1,0:T(8,128)(2,1)} %refs_0_.1, bf16[2,32,32]{2,1,0:T(8,128)(2,1)} %refs_1_.1, bf16[2,32,32]{2,1,0:T(8,128)(2,1)} %refs_2_.1, f32[1,32]{1,0:T(1,128)} %bitcast.6, f32[1,32]{1,0:T(1,128)} %bitcast.7, bf16[4,5,4,4096]{3,2,1,0:T(4,128)(2,1)} %bitcast.5, ...), custom_call_target="tpu_custom_call" | custom-call | flops 167772160 | bytes 524288 | tf_op jit(solution)/shard_map/pallas_call | solution.py:489
  26.8 1.7 %copy.14 = bf16[4,4,64,128]{3,2,1,0:T(8,128)(2,1)} copy(bf16[4,4,64,128]{3,2,1,0:T(8,128)(2,1)} %shard_map.118) | data formatting | bytes 524288

commit v3 on v2

--- a/solution.py
+++ b/solution.py
@@ -84,6 +84,7 @@
     halo_send_sem,
     halo_recv_sem,
     fetch_sem,
+    route,
     ) = refs
     fetches = [
         pltpu.make_async_copy(src, dst, fetch_sem.at[k])
@@ -138,7 +139,7 @@
         halo_cols[:, 1] = zero_side
 
     for k in range(12):
-        if k != 5:
+        if k not in (0, 5):
             fetches[k].wait()
 
     table[...] = jnp.zeros_like(table)
@@ -157,6 +158,8 @@
         bias_table[2:3, span] = bias_mix[...]
     taps = table[:, : 2 * feats].astype(BF16)
     mixes = [table[:, (2 + h) * feats : (3 + h) * feats].astype(BF16) for h in range(3)]
+    early_mix = jnp.concatenate(mixes[:2], axis=0)
+    late_mix = jnp.concatenate([mixes[2], mixes[2]], axis=0)
 
     def gate(block_rows):
         pre = dot(block_rows, taps)
@@ -173,13 +176,11 @@
         edge_tiles[e, :half] = pairs.astype(BF16)
         edge_tiles[e, half:] = pltpu.roll(pairs, size, 1).astype(BF16)
 
-    def slots(d):
-        head, tail = jnp.int32(-1), jnp.int32(-1)
-        for e in range(edges):
-            hit = out_dev[0, 0, e] == d
-            head = jnp.where(hit & (head < 0), e, head)
-            tail = jnp.where(hit, e, tail)
-        return ((jnp.maximum(head, 0), head >= 0), (jnp.maximum(tail, 0), tail != head))
+    part = n // 2
+
+    def destination(k):
+        side = (rx // part + 1 + k // part) % 2
+        return side * part + (rx % part + k % part + 1) % part
 
     lane = lax.broadcasted_iota(jnp.int32, (8, CAP * size), 1)
 
@@ -224,53 +225,63 @@
             device_id_type=MESH,
         )
 
-    part = n // 2
-
-    def destination(k):
-        side = (rx // part + 1 + k // part) % 2
-        return side * part + (rx % part + k % part + 1) % part
-
-    def send_far(signal, hop):
-        def one(k):
-            d = destination(k)
-            picked, targets = [], []
-            for index, valid in slots(d):
-                b = out_block[0, 0, index]
-                block = signal[lax.div(b, bc), lax.rem(b, bc)]
-                picked.append((index, valid, block))
-                targets.append(jnp.where(valid, out_target[0, 0, index], -1))
-            if hop == 0:
-                both = gate(jnp.concatenate([block for _, _, block in picked], axis=0))
-                values = [both[c * size : (c + 1) * size] for c in range(CAP)]
+    def find_route(k):
+        d = destination(k)
+        head, tail = jnp.int32(-1), jnp.int32(-1)
+        for e in range(edges):
+            hit = out_dev[0, 0, e] == d
+            head = jnp.where(hit & (head < 0), e, head)
+            tail = jnp.where(hit, e, tail)
+        found = ((head, head >= 0), (tail, tail != head))
+        for c, (index, valid) in enumerate(found):
+            index = jnp.maximum(index, 0)
+            route[k, c] = index
+            route[k, CAP + c] = out_block[0, 0, index]
+            route[k, 2 * CAP + c] = jnp.where(valid, 1, 0)
+
+    def send_targets(k, own):
+        d = destination(k)
+        names = [
+            jnp.where(route[k, 2 * CAP + c] == 1, out_target[0, 0, route[k, c]], -1)
+            for c in range(CAP)
+        ]
+        named = jnp.where(lane < size, names[0], names[1]).astype(F32)
+        if own:
+            target_recv[rx] = named
+        else:
+            target_send[d] = named
+            target_copy(d, rx).start()
+
+    team = 4
+
+    def send_group(signal, hop, start, last, gating):
+        ks = [start + g for g in range(team)]
+        picked = []
+        for k in ks:
+            for c in range(CAP):
+                b = route[k, CAP + c]
+                picked.append(signal[lax.div(b, bc), lax.rem(b, bc)])
+        if gating:
+            gates = gate(jnp.concatenate(picked, axis=0))
+            picked = [gates[p * size : (p + 1) * size] for p in range(team * CAP)]
+        sums = []
+        for g, k in enumerate(ks):
+            for c in range(CAP):
+                product = dot(edge_tiles[route[k, c]][:, :size], picked[g * CAP + c])
+                sums.append((product * route[k, 2 * CAP + c].astype(F32)).astype(BF16))
+        for g, k in enumerate(ks):
+            both = jnp.concatenate(sums[g * CAP : (g + 1) * CAP], axis=0)
+            if last and g == team - 1:
+                recv_buf[hop, rx] = both
             else:
-                values = [block for _, _, block in picked]
-            products = []
-            for (index, valid, _), block in zip(picked, values):
-                product = dot(edge_tiles[index][:, :size], block)
-                products.append((product * jnp.where(valid, 1.0, 0.0)).astype(BF16))
-            both = jnp.concatenate(products, axis=0)
-            named = jnp.where(lane < size, targets[0], targets[1]).astype(F32)
-            own = k == n - 1
-
-            def keep():
-                recv_buf[hop, rx] = both
-                if hop == 0:
-                    target_recv[rx] = named
-
-            def send():
-                send_buf[hop, d] = both
-                far_copy(hop, d, rx).start()
-                if hop == 0:
-                    target_send[d] = named
-                    target_copy(d, rx).start()
-
-            if isinstance(own, bool):
-                keep() if own else send()
-            else:
-                pl.when(own)(keep)
-                pl.when(jnp.logical_not(own))(send)
-
-        each(n, one)
+                send_buf[hop, destination(k)] = both
+        for g, k in enumerate(ks):
+            if not (last and g == team - 1):
+                far_copy(hop, destination(k), rx).start()
+
+    def send_rest(signal, hop):
+        each(n // team - 2, lambda g: send_group(signal, hop, (g + 1) * team, False, False))
+        send_group(signal, hop, n - team, True, False)
 
     part_pairs = n // 4
 
@@ -314,6 +325,7 @@
                 acc[pl.ds(at, half, stride=2), :] = total[:half]
                 acc[pl.ds(at + 1, half, stride=2), :] = total[half:]
 
+    each(n, find_route)
     pl.semaphore_wait(
         barrier,
         n - 1 + jnp.where(ry > 0, 1, 0) + jnp.where(ry < ny - 1, 1, 0),
@@ -327,10 +339,14 @@
         for sends, gets, copy in halo_copies(signal, hop):
             pl.when(gets)(copy.wait_recv)
 
-    send_far(cell, 0)
+    each(n - 1, lambda k: send_targets(k, False))
+    send_targets(n - 1, True)
+    fetches[0].wait()
+    send_group(cell, 0, 0, False, True)
     for i in range(br):
         gated[i] = gate(cell[i].reshape(bc * size, feats)).reshape(bc, size, feats)
     start_halo(gated, 0)
+    send_rest(gated, 0)
 
     low = lax.broadcasted_iota(jnp.int32, (half, 2 * size), 1) < size
 
@@ -383,12 +399,13 @@
         first[i] = total.astype(BF16).reshape(bc, size, feats)
 
     add_far(0, end_first)
-    send_far(first, 1)
+    send_group(first, 1, 0, False, False)
     start_halo(first, 1)
+    send_rest(first, 1)
 
     for i in range(br):
-        own = dot(gated[i].reshape(strip, feats), mixes[0])
-        own = own + dot(first[i].reshape(strip, feats), mixes[1]) + bias_table[2:3]
+        known = [gated[i].reshape(strip, feats), first[i].reshape(strip, feats)]
+        own = dot(jnp.concatenate(known, axis=1), early_mix) + bias_table[2:3]
         base[i * strip : (i + 1) * strip] = own + cell[i].reshape(strip, feats).astype(F32)
     wait_halo(first, 1)
     near(first, 1)
@@ -397,7 +414,7 @@
         upper = second.astype(BF16)
         lower = (second - upper.astype(F32)).astype(BF16)
         total = base[i * strip : (i + 1) * strip]
-        total = total + (dot(upper, mixes[2]) + dot(lower, mixes[2]))
+        total = total + dot(jnp.concatenate([upper, lower], axis=1), late_mix)
         out[i] = total.astype(BF16).reshape(bc, size, feats)
 
     add_far(1, end_second)
@@ -484,6 +501,7 @@
         dma((2, 2, 2)),
         dma((2, 2, 2)),
         dma((12,)),
+        pltpu.SMEM((n, 3 * CAP), jnp.int32),
     ]
     near_flops = 2 * 2 * 5 * rows * size * feats
     return pl.pallas_call(
@@ -496,9 +514,9 @@
             flops=near_flops, bytes_accessed=2 * rows * feats * 2, transcendentals=2 * rows * feats
         ),
         compiler_params=pltpu.CompilerParams(
-            collective_id=0, has_side_effects=True, vmem_limit_bytes=63 * 1024 * 1024
+            collective_id=0, has_side_effects=True, vmem_limit_bytes=40 * 1024 * 1024
         ),
-    )(*operands)
+    )(*(pltpu.with_memory_space_constraint(a, pltpu.HBM) for a in operands))
 
 
 def solution(mesh):

time: 28.9 us -> 25.9 us (0.90)
  Pallas kernels: 26.8 us -> 24.9 us
  local copies, waits for them, and re-layouts: 1.67 us -> 0.71 us
    pallas_call x1, Pallas kernels: 26.8 us -> 24.9 us  [local(): pl.pallas_call(functools.partial(kernel, n, ny), out_shape=jax.ShapeDtype...]
    unnamed x1, local copies, waits for them, and re-layouts: 1.67 us -> 0.71 us
where the time goes in v3:
time: 25.9 us; the launch traced here: 25.6 us
  Pallas kernels  24.9 us (96%)
  local copies, waits for them, and re-layouts  0.71 us (3%)
    pallas_call x1, Pallas kernels, local(): pl.pallas_call(functools.partial(kernel, n, ny), out_shape=jax.ShapeDtype...  24.9 us
    unnamed x1, local copies, waits for them, and re-layouts  0.71 us

profile of v3, /device:TPU:0, one launch (start us, length us, event | category | flops | bytes accessed | tf_op | source)
XLA Modules:
  0.0 25.6 jit_solution(13161929666120172795)
XLA Ops:
  0.0 24.9 %shard_map.118 = bf16[4,4,64,128]{3,2,1,0:T(8,128)(2,1)S(1)} custom-call(bf16[4,4,64,128]{3,2,1,0:T(8,128)(2,1)} %refs_0_.1, bf16[2,32,32]{2,1,0:T(8,128)(2,1)} %refs_1_.1, bf16[2,32,32]{2,1,0:T(8,128)(2,1)} %refs_2_.1, f32[1,32]{1,0:T(1,128)} %bitcast.6, f32[1,32]{1,0:T(1,128)} %bitcast.7, bf16[4,5,4,4096]{3,2,1,0:T(4,128)(2,1)} %bitcast.5, ...), custom_call_target="tpu_custom_call" | custom-call | flops 167772160 | bytes 524288 | tf_op jit(solution)/shard_map/pallas_call | solution.py:507
  24.9 0.7 %copy.14 = bf16[4,4,64,128]{3,2,1,0:T(8,128)(2,1)} copy(bf16[4,4,64,128]{3,2,1,0:T(8,128)(2,1)S(1)} %shard_map.118) | data formatting | bytes 524288

commit v4 on v3

--- a/solution.py
+++ b/solution.py
@@ -254,16 +254,13 @@
 
     team = 4
 
-    def send_group(signal, hop, start, last, gating):
+    def send_group(signal, hop, start, last):
         ks = [start + g for g in range(team)]
         picked = []
         for k in ks:
             for c in range(CAP):
                 b = route[k, CAP + c]
                 picked.append(signal[lax.div(b, bc), lax.rem(b, bc)])
-        if gating:
-            gates = gate(jnp.concatenate(picked, axis=0))
-            picked = [gates[p * size : (p + 1) * size] for p in range(team * CAP)]
         sums = []
         for g, k in enumerate(ks):
             for c in range(CAP):
@@ -279,9 +276,9 @@
             if not (last and g == team - 1):
                 far_copy(hop, destination(k), rx).start()
 
-    def send_rest(signal, hop):
-        each(n // team - 2, lambda g: send_group(signal, hop, (g + 1) * team, False, False))
-        send_group(signal, hop, n - team, True, False)
+    def send_far(signal, hop):
+        each(n // team - 1, lambda g: send_group(signal, hop, g * team, False))
+        send_group(signal, hop, n - team, True)
 
     part_pairs = n // 4
 
@@ -342,11 +339,10 @@
     each(n - 1, lambda k: send_targets(k, False))
     send_targets(n - 1, True)
     fetches[0].wait()
-    send_group(cell, 0, 0, False, True)
     for i in range(br):
         gated[i] = gate(cell[i].reshape(bc * size, feats)).reshape(bc, size, feats)
     start_halo(gated, 0)
-    send_rest(gated, 0)
+    send_far(gated, 0)
 
     low = lax.broadcasted_iota(jnp.int32, (half, 2 * size), 1) < size
 
@@ -399,9 +395,8 @@
         first[i] = total.astype(BF16).reshape(bc, size, feats)
 
     add_far(0, end_first)
-    send_group(first, 1, 0, False, False)
     start_halo(first, 1)
-    send_rest(first, 1)
+    send_far(first, 1)
 
     for i in range(br):
         known = [gated[i].reshape(strip, feats), first[i].reshape(strip, feats)]

time: 25.9 us -> 24.8 us (0.958)
  Pallas kernels: 24.9 us -> 23.8 us
    pallas_call x1, Pallas kernels: 24.9 us -> 23.8 us  [local(): pl.pallas_call(functools.partial(kernel, n, ny), out_shape=jax.ShapeDtype...]
where the time goes in v4:
time: 24.8 us; the launch traced here: 24.5 us
  Pallas kernels  23.8 us (96%)
  local copies, waits for them, and re-layouts  0.71 us (3%)
    pallas_call x1, Pallas kernels, local(): pl.pallas_call(functools.partial(kernel, n, ny), out_shape=jax.ShapeDtype...  23.8 us
    unnamed x1, local copies, waits for them, and re-layouts  0.71 us

profile of v4, /device:TPU:0, one launch (start us, length us, event | category | flops | bytes accessed | tf_op | source)
XLA Modules:
  0.0 24.5 jit_solution(10406898401207425968)
XLA Ops:
  0.0 23.8 %shard_map.118 = bf16[4,4,64,128]{3,2,1,0:T(8,128)(2,1)S(1)} custom-call(bf16[4,4,64,128]{3,2,1,0:T(8,128)(2,1)} %refs_0_.1, bf16[2,32,32]{2,1,0:T(8,128)(2,1)} %refs_1_.1, bf16[2,32,32]{2,1,0:T(8,128)(2,1)} %refs_2_.1, f32[1,32]{1,0:T(1,128)} %bitcast.6, f32[1,32]{1,0:T(1,128)} %bitcast.7, bf16[4,5,4,4096]{3,2,1,0:T(4,128)(2,1)} %bitcast.5, ...), custom_call_target="tpu_custom_call" | custom-call | flops 167772160 | bytes 524288 | tf_op jit(solution)/shard_map/pallas_call | solution.py:502
  23.8 0.7 %copy.14 = bf16[4,4,64,128]{3,2,1,0:T(8,128)(2,1)} copy(bf16[4,4,64,128]{3,2,1,0:T(8,128)(2,1)S(1)} %shard_map.118) | data formatting | bytes 524288

commit v5 on v4

--- a/solution.py
+++ b/solution.py
@@ -90,7 +90,7 @@
         pltpu.make_async_copy(src, dst, fetch_sem.at[k])
         for k, (src, dst) in enumerate(zip(inputs, landing))
     ]
-    for k in (1, 2, 3, 4, 9, 6, 7, 8, 0, 10, 11, 5):
+    for k in (1, 2, 3, 4, 0, 9, 6, 7, 8, 10, 11, 5):
         fetches[k].start()
     br, bc, size, feats = cell.shape
     blocks = br * bc
@@ -120,27 +120,64 @@
     def _():
         pl.semaphore_signal(barrier, inc=1, device_id={"ry": ry + 1}, device_id_type=MESH)
 
+    def halo_copies(signal, hop):
+        sides = []
+        for which, (axis, here, count, halo) in enumerate(
+            (("rx", rx, n, halo_rows), ("ry", ry, ny, halo_cols))
+        ):
+            last = (br if which == 0 else bc) - 1
+            for side, (edge, step) in enumerate(((last, 1), (0, -1))):
+                src = signal.at[edge] if which == 0 else signal.at[:, edge]
+                copy = pltpu.make_async_remote_copy(
+                    src_ref=src,
+                    dst_ref=halo.at[2 - hop, side],
+                    send_sem=halo_send_sem.at[hop, which, side],
+                    recv_sem=halo_recv_sem.at[hop, which, side],
+                    device_id={axis: jnp.clip(here + step, 0, count - 1)},
+                    device_id_type=MESH,
+                )
+                sends = (here < count - 1) if step == 1 else (here > 0)
+                gets = (here > 0) if step == 1 else (here < count - 1)
+                sides.append((sends, gets, copy))
+        return sides
+
+    def start_halo(signal, hop, axes=(0, 1)):
+        for which in axes:
+            for sends, gets, copy in halo_copies(signal, hop)[2 * which : 2 * which + 2]:
+                pl.when(sends)(copy.start)
+
+    def wait_halo(signal, hop):
+        for sends, gets, copy in halo_copies(signal, hop):
+            pl.when(gets)(copy.wait_recv)
+
+    pl.semaphore_wait(
+        barrier,
+        n - 1 + jnp.where(ry > 0, 1, 0) + jnp.where(ry < ny - 1, 1, 0),
+    )
+
     zero_side = jnp.zeros((2,) + halo_rows.shape[2:], BF16)
 
     @pl.when(rx == 0)
     def _():
-        halo_rows[:, 0] = zero_side
+        halo_rows[1:, 0] = zero_side
 
     @pl.when(rx == n - 1)
     def _():
-        halo_rows[:, 1] = zero_side
+        halo_rows[1:, 1] = zero_side
 
     @pl.when(ry == 0)
     def _():
-        halo_cols[:, 0] = zero_side
+        halo_cols[1:, 0] = zero_side
 
     @pl.when(ry == ny - 1)
     def _():
-        halo_cols[:, 1] = zero_side
-
-    for k in range(12):
-        if k not in (0, 5):
-            fetches[k].wait()
+        halo_cols[1:, 1] = zero_side
+
+    start_halo(inputs[0], 0)
+    for k in range(1, 5):
+        fetches[k].wait()
+    for k in (10, 11):
+        fetches[k].wait()
 
     table[...] = jnp.zeros_like(table)
     for t in range(steps):
@@ -168,6 +205,13 @@
         value = jnp.tanh(pre_f) * (0.5 * jnp.tanh(0.5 * pre_g) + 0.5)
         return value.astype(BF16)
 
+    fetches[0].wait()
+    for i in range(br):
+        gated[i] = gate(cell[i].reshape(bc * size, feats)).reshape(bc, size, feats)
+
+    for k in range(6, 10):
+        fetches[k].wait()
+
     for r in range(half):
         piece = out_tiles[0, 0, :, r * 2 * size : (r + 1) * 2 * size]
         edge_spread[r * stride : r * stride + edges] = piece.astype(F32)
@@ -182,28 +226,7 @@
         side = (rx // part + 1 + k // part) % 2
         return side * part + (rx % part + k % part + 1) % part
 
-    lane = lax.broadcasted_iota(jnp.int32, (8, CAP * size), 1)
-
-    def halo_copies(signal, hop):
-        sides = []
-        for which, (axis, here, count, halo) in enumerate(
-            (("rx", rx, n, halo_rows), ("ry", ry, ny, halo_cols))
-        ):
-            last = (br if which == 0 else bc) - 1
-            for side, (edge, step) in enumerate(((last, 1), (0, -1))):
-                src = signal.at[edge] if which == 0 else signal.at[:, edge]
-                copy = pltpu.make_async_remote_copy(
-                    src_ref=src,
-                    dst_ref=halo.at[hop, side],
-                    send_sem=halo_send_sem.at[hop, which, side],
-                    recv_sem=halo_recv_sem.at[hop, which, side],
-                    device_id={axis: jnp.clip(here + step, 0, count - 1)},
-                    device_id_type=MESH,
-                )
-                sends = (here < count - 1) if step == 1 else (here > 0)
-                gets = (here > 0) if step == 1 else (here < count - 1)
-                sides.append((sends, gets, copy))
-        return sides
+    lane = lax.broadcasted_iota(jnp.int32, (1, CAP * size), 1)
 
     def far_copy(hop, d, source):
         return pltpu.make_async_remote_copy(
@@ -297,7 +320,7 @@
                 wait_source(2 * pair)
                 wait_source(2 * pair + 1)
             landed = recv_buf[hop, pl.ds(2 * pair, 2)].reshape(2 * CAP * size, feats)
-            for i in range(br):
+            for i in (0, br - 1, *range(1, br - 1)):
                 span = slice(i * strip, (i + 1) * strip)
                 total = acc[span] + dot(select[pair, span], landed)
                 if isinstance(q, int) and q == n // 2 - 1:
@@ -323,25 +346,8 @@
                 acc[pl.ds(at + 1, half, stride=2), :] = total[half:]
 
     each(n, find_route)
-    pl.semaphore_wait(
-        barrier,
-        n - 1 + jnp.where(ry > 0, 1, 0) + jnp.where(ry < ny - 1, 1, 0),
-    )
-
-    def start_halo(signal, hop):
-        for sends, gets, copy in halo_copies(signal, hop):
-            pl.when(sends)(copy.start)
-
-    def wait_halo(signal, hop):
-        for sends, gets, copy in halo_copies(signal, hop):
-            pl.when(gets)(copy.wait_recv)
-
     each(n - 1, lambda k: send_targets(k, False))
     send_targets(n - 1, True)
-    fetches[0].wait()
-    for i in range(br):
-        gated[i] = gate(cell[i].reshape(bc * size, feats)).reshape(bc, size, feats)
-    start_halo(gated, 0)
     send_far(gated, 0)
 
     low = lax.broadcasted_iota(jnp.int32, (half, 2 * size), 1) < size
@@ -371,7 +377,13 @@
     fetches[5].wait()
     blocks_loop(br, arrange, 2)
 
-    wait_halo(gated, 0)
+    wait_halo(inputs[0], 0)
+    inside = ((rx > 0, rx < n - 1), (ry > 0, ry < ny - 1))
+    for which, halo in enumerate((halo_rows, halo_cols)):
+        for side in range(2):
+            values = gate(halo[2, side].reshape(bc * size, feats))
+            kept = values * jnp.where(inside[which][side], 1.0, 0.0).astype(BF16)
+            halo[0, side] = kept.reshape(bc, size, feats)
     near(gated, 0)
 
     def wait_target(k):
@@ -393,9 +405,11 @@
 
     def end_first(i, total):
         first[i] = total.astype(BF16).reshape(bc, size, feats)
+        if i == br - 1:
+            start_halo(first, 1, (0,))
 
     add_far(0, end_first)
-    start_halo(first, 1)
+    start_halo(first, 1, (1,))
     send_far(first, 1)
 
     for i in range(br):
@@ -414,7 +428,7 @@
 
     add_far(1, end_second)
 
-    for hop, signal in enumerate((gated, first)):
+    for hop, signal in enumerate((inputs[0], first)):
         for sends, gets, copy in halo_copies(signal, hop):
             pl.when(sends)(copy.wait_send)
 
@@ -474,12 +488,12 @@
     ] + [
         pltpu.VMEM((br, bc, size, feats), BF16),
         pltpu.VMEM((br, bc, size, feats), BF16),
-        pltpu.VMEM((2, 2, bc, size, feats), BF16),
-        pltpu.VMEM((2, 2, br, size, feats), BF16),
+        pltpu.VMEM((3, 2, bc, size, feats), BF16),
+        pltpu.VMEM((3, 2, br, size, feats), BF16),
         pltpu.VMEM((2, n, CAP * size, feats), BF16),
         pltpu.VMEM((2, n, CAP * size, feats), BF16),
-        pltpu.VMEM((n, 8, CAP * size), F32),
-        pltpu.VMEM((n, 8, CAP * size), F32),
+        pltpu.VMEM((n, 1, CAP * size), F32),
+        pltpu.VMEM((n, 1, CAP * size), F32),
         pltpu.VMEM((n // 2, rows, 2 * CAP * size), BF16),
         pltpu.VMEM((blocks, size, 6 * size), BF16),
         pltpu.VMEM((edges, size, 2 * size), BF16),

time: 24.8 us -> 24.9 us (level)
  Pallas kernels: 23.8 us -> 24.1 us
where the time goes in v5:
time: 24.9 us; the launch traced here: 24.8 us
  Pallas kernels  24.1 us (97%)
  local copies, waits for them, and re-layouts  0.71 us (3%)
    pallas_call x1, Pallas kernels, local(): pl.pallas_call(functools.partial(kernel, n, ny), out_shape=jax.ShapeDtype...  24.1 us
    unnamed x1, local copies, waits for them, and re-layouts  0.71 us

profile of v5, /device:TPU:0, one launch (start us, length us, event | category | flops | bytes accessed | tf_op | source)
XLA Modules:
  0.0 24.8 jit_solution(4388780633473689482)
XLA Ops:
  0.0 24.1 %shard_map.118 = bf16[4,4,64,128]{3,2,1,0:T(8,128)(2,1)S(1)} custom-call(bf16[4,4,64,128]{3,2,1,0:T(8,128)(2,1)} %refs_0_.1, bf16[2,32,32]{2,1,0:T(8,128)(2,1)} %refs_1_.1, bf16[2,32,32]{2,1,0:T(8,128)(2,1)} %refs_2_.1, f32[1,32]{1,0:T(1,128)} %bitcast.6, f32[1,32]{1,0:T(1,128)} %bitcast.7, bf16[4,5,4,4096]{3,2,1,0:T(4,128)(2,1)} %bitcast.5, ...), custom_call_target="tpu_custom_call" | custom-call | flops 167772160 | bytes 524288 | tf_op jit(solution)/shard_map/pallas_call | solution.py:516
  24.1 0.7 %copy.14 = bf16[4,4,64,128]{3,2,1,0:T(8,128)(2,1)} copy(bf16[4,4,64,128]{3,2,1,0:T(8,128)(2,1)S(1)} %shard_map.118) | data formatting | bytes 524288

commit v6 on v5

--- a/solution.py
+++ b/solution.py
@@ -90,7 +90,7 @@
         pltpu.make_async_copy(src, dst, fetch_sem.at[k])
         for k, (src, dst) in enumerate(zip(inputs, landing))
     ]
-    for k in (1, 2, 3, 4, 0, 9, 6, 7, 8, 10, 11, 5):
+    for k in (6, 7, 8, 1, 2, 3, 4, 9, 0, 10, 11, 5):
         fetches[k].start()
     br, bc, size, feats = cell.shape
     blocks = br * bc
@@ -130,7 +130,7 @@
                 src = signal.at[edge] if which == 0 else signal.at[:, edge]
                 copy = pltpu.make_async_remote_copy(
                     src_ref=src,
-                    dst_ref=halo.at[2 - hop, side],
+                    dst_ref=halo.at[2 - hop if which == 0 else hop, side],
                     send_sem=halo_send_sem.at[hop, which, side],
                     recv_sem=halo_recv_sem.at[hop, which, side],
                     device_id={axis: jnp.clip(here + step, 0, count - 1)},
@@ -146,9 +146,10 @@
             for sends, gets, copy in halo_copies(signal, hop)[2 * which : 2 * which + 2]:
                 pl.when(sends)(copy.start)
 
-    def wait_halo(signal, hop):
-        for sends, gets, copy in halo_copies(signal, hop):
-            pl.when(gets)(copy.wait_recv)
+    def wait_halo(signal, hop, axes=(0, 1)):
+        for which in axes:
+            for sends, gets, copy in halo_copies(signal, hop)[2 * which : 2 * which + 2]:
+                pl.when(gets)(copy.wait_recv)
 
     pl.semaphore_wait(
         barrier,
@@ -167,16 +168,14 @@
 
     @pl.when(ry == 0)
     def _():
-        halo_cols[1:, 0] = zero_side
+        halo_cols[:, 0] = zero_side
 
     @pl.when(ry == ny - 1)
     def _():
-        halo_cols[1:, 1] = zero_side
-
-    start_halo(inputs[0], 0)
+        halo_cols[:, 1] = zero_side
+
+    start_halo(inputs[0], 0, (0,))
     for k in range(1, 5):
-        fetches[k].wait()
-    for k in (10, 11):
         fetches[k].wait()
 
     table[...] = jnp.zeros_like(table)
@@ -187,16 +186,9 @@
                 if to < steps:
                     at = which * feats + to * channels
                     table[span, at : at + channels] = weights[tap].astype(F32)
-        for hop in range(3):
-            at = (2 + hop) * feats + t * channels
-            table[span, at : at + channels] = w_mix[hop].astype(F32)
         bias_table[0:1, span] = bias_filter[...]
         bias_table[1:2, span] = bias_gate[...]
-        bias_table[2:3, span] = bias_mix[...]
     taps = table[:, : 2 * feats].astype(BF16)
-    mixes = [table[:, (2 + h) * feats : (3 + h) * feats].astype(BF16) for h in range(3)]
-    early_mix = jnp.concatenate(mixes[:2], axis=0)
-    late_mix = jnp.concatenate([mixes[2], mixes[2]], axis=0)
 
     def gate(block_rows):
         pre = dot(block_rows, taps)
@@ -204,10 +196,6 @@
         pre_g = pre[:, feats:] + bias_table[1:2]
         value = jnp.tanh(pre_f) * (0.5 * jnp.tanh(0.5 * pre_g) + 0.5)
         return value.astype(BF16)
-
-    fetches[0].wait()
-    for i in range(br):
-        gated[i] = gate(cell[i].reshape(bc * size, feats)).reshape(bc, size, feats)
 
     for k in range(6, 10):
         fetches[k].wait()
@@ -277,13 +265,16 @@
 
     team = 4
 
-    def send_group(signal, hop, start, last):
+    def send_group(signal, hop, start, last, gating):
         ks = [start + g for g in range(team)]
         picked = []
         for k in ks:
             for c in range(CAP):
                 b = route[k, CAP + c]
                 picked.append(signal[lax.div(b, bc), lax.rem(b, bc)])
+        if gating:
+            gates = gate(jnp.concatenate(picked, axis=0))
+            picked = [gates[p * size : (p + 1) * size] for p in range(team * CAP)]
         sums = []
         for g, k in enumerate(ks):
             for c in range(CAP):
@@ -299,9 +290,9 @@
             if not (last and g == team - 1):
                 far_copy(hop, destination(k), rx).start()
 
-    def send_far(signal, hop):
-        each(n // team - 1, lambda g: send_group(signal, hop, g * team, False))
-        send_group(signal, hop, n - team, True)
+    def send_rest(signal, hop):
+        each(n // team - 2, lambda g: send_group(signal, hop, (g + 1) * team, False, False))
+        send_group(signal, hop, n - team, True, False)
 
     part_pairs = n // 4
 
@@ -346,9 +337,14 @@
                 acc[pl.ds(at + 1, half, stride=2), :] = total[half:]
 
     each(n, find_route)
+    fetches[0].wait()
+    send_group(cell, 0, 0, False, True)
+    for i in range(br):
+        gated[i] = gate(cell[i].reshape(bc * size, feats)).reshape(bc, size, feats)
+    start_halo(gated, 0, (1,))
+    send_rest(gated, 0)
     each(n - 1, lambda k: send_targets(k, False))
     send_targets(n - 1, True)
-    send_far(gated, 0)
 
     low = lax.broadcasted_iota(jnp.int32, (half, 2 * size), 1) < size
 
@@ -377,13 +373,12 @@
     fetches[5].wait()
     blocks_loop(br, arrange, 2)
 
-    wait_halo(inputs[0], 0)
-    inside = ((rx > 0, rx < n - 1), (ry > 0, ry < ny - 1))
-    for which, halo in enumerate((halo_rows, halo_cols)):
-        for side in range(2):
-            values = gate(halo[2, side].reshape(bc * size, feats))
-            kept = values * jnp.where(inside[which][side], 1.0, 0.0).astype(BF16)
-            halo[0, side] = kept.reshape(bc, size, feats)
+    wait_halo(inputs[0], 0, (0,))
+    for side, inside in enumerate((rx > 0, rx < n - 1)):
+        values = gate(halo_rows[2, side].reshape(bc * size, feats))
+        kept = values * jnp.where(inside, 1.0, 0.0).astype(BF16)
+        halo_rows[0, side] = kept.reshape(bc, size, feats)
+    wait_halo(gated, 0, (1,))
     near(gated, 0)
 
     def wait_target(k):
@@ -410,7 +405,20 @@
 
     add_far(0, end_first)
     start_halo(first, 1, (1,))
-    send_far(first, 1)
+    send_group(first, 1, 0, False, False)
+    send_rest(first, 1)
+
+    for k in (10, 11):
+        fetches[k].wait()
+    for t in range(steps):
+        span = slice(t * channels, (t + 1) * channels)
+        for hop in range(3):
+            at = (2 + hop) * feats + t * channels
+            table[span, at : at + channels] = w_mix[hop].astype(F32)
+        bias_table[2:3, span] = bias_mix[...]
+    mixes = [table[:, (2 + h) * feats : (3 + h) * feats].astype(BF16) for h in range(3)]
+    early_mix = jnp.concatenate(mixes[:2], axis=0)
+    late_mix = jnp.concatenate([mixes[2], mixes[2]], axis=0)
 
     for i in range(br):
         known = [gated[i].reshape(strip, feats), first[i].reshape(strip, feats)]
@@ -428,9 +436,10 @@
 
     add_far(1, end_second)
 
-    for hop, signal in enumerate((inputs[0], first)):
-        for sends, gets, copy in halo_copies(signal, hop):
-            pl.when(sends)(copy.wait_send)
+    for hop, signals in enumerate(((inputs[0], gated), (first, first))):
+        for which in range(2):
+            for sends, gets, copy in halo_copies(signals[which], hop)[2 * which : 2 * which + 2]:
+                pl.when(sends)(copy.wait_send)
 
         def sent(k):
             d = destination(k)
@@ -489,7 +498,7 @@
         pltpu.VMEM((br, bc, size, feats), BF16),
         pltpu.VMEM((br, bc, size, feats), BF16),
         pltpu.VMEM((3, 2, bc, size, feats), BF16),
-        pltpu.VMEM((3, 2, br, size, feats), BF16),
+        pltpu.VMEM((2, 2, br, size, feats), BF16),
         pltpu.VMEM((2, n, CAP * size, feats), BF16),
         pltpu.VMEM((2, n, CAP * size, feats), BF16),
         pltpu.VMEM((n, 1, CAP * size), F32),

time: 24.9 us -> 26.4 us (1.060)
  Pallas kernels: 24.1 us -> 25.5 us
    pallas_call x1, Pallas kernels: 24.1 us -> 25.5 us  [local(): pl.pallas_call(functools.partial(kernel, n, ny), out_shape=jax.ShapeDtype...]
where the time goes in v6:
time: 26.4 us; the launch traced here: 26.2 us
  Pallas kernels  25.5 us (97%)
  local copies, waits for them, and re-layouts  0.71 us (3%)
    pallas_call x1, Pallas kernels, local(): pl.pallas_call(functools.partial(kernel, n, ny), out_shape=jax.ShapeDtype...  25.5 us
    unnamed x1, local copies, waits for them, and re-layouts  0.71 us

profile of v6, /device:TPU:0, one launch (start us, length us, event | category | flops | bytes accessed | tf_op | source)
XLA Modules:
  0.0 26.2 jit_solution(6287455563649385697)
XLA Ops:
  0.0 25.5 %shard_map.118 = bf16[4,4,64,128]{3,2,1,0:T(8,128)(2,1)S(1)} custom-call(bf16[4,4,64,128]{3,2,1,0:T(8,128)(2,1)} %refs_0_.1, bf16[2,32,32]{2,1,0:T(8,128)(2,1)} %refs_1_.1, bf16[2,32,32]{2,1,0:T(8,128)(2,1)} %refs_2_.1, f32[1,32]{1,0:T(1,128)} %bitcast.6, f32[1,32]{1,0:T(1,128)} %bitcast.7, bf16[4,5,4,4096]{3,2,1,0:T(4,128)(2,1)} %bitcast.5, ...), custom_call_target="tpu_custom_call" | custom-call | flops 167772160 | bytes 524288 | tf_op jit(solution)/shard_map/pallas_call | solution.py:525
  25.5 0.7 %copy.14 = bf16[4,4,64,128]{3,2,1,0:T(8,128)(2,1)} copy(bf16[4,4,64,128]{3,2,1,0:T(8,128)(2,1)S(1)} %shard_map.118) | data formatting | bytes 524288

commit v7 on v6

--- a/solution.py
+++ b/solution.py
@@ -265,16 +265,13 @@
 
     team = 4
 
-    def send_group(signal, hop, start, last, gating):
+    def send_group(signal, hop, start, last):
         ks = [start + g for g in range(team)]
         picked = []
         for k in ks:
             for c in range(CAP):
                 b = route[k, CAP + c]
                 picked.append(signal[lax.div(b, bc), lax.rem(b, bc)])
-        if gating:
-            gates = gate(jnp.concatenate(picked, axis=0))
-            picked = [gates[p * size : (p + 1) * size] for p in range(team * CAP)]
         sums = []
         for g, k in enumerate(ks):
             for c in range(CAP):
@@ -290,9 +287,9 @@
             if not (last and g == team - 1):
                 far_copy(hop, destination(k), rx).start()
 
-    def send_rest(signal, hop):
-        each(n // team - 2, lambda g: send_group(signal, hop, (g + 1) * team, False, False))
-        send_group(signal, hop, n - team, True, False)
+    def send_far(signal, hop):
+        each(n // team - 1, lambda g: send_group(signal, hop, g * team, False))
+        send_group(signal, hop, n - team, True)
 
     part_pairs = n // 4
 
@@ -337,14 +334,13 @@
                 acc[pl.ds(at + 1, half, stride=2), :] = total[half:]
 
     each(n, find_route)
+    each(n - 1, lambda k: send_targets(k, False))
+    send_targets(n - 1, True)
     fetches[0].wait()
-    send_group(cell, 0, 0, False, True)
     for i in range(br):
         gated[i] = gate(cell[i].reshape(bc * size, feats)).reshape(bc, size, feats)
     start_halo(gated, 0, (1,))
-    send_rest(gated, 0)
-    each(n - 1, lambda k: send_targets(k, False))
-    send_targets(n - 1, True)
+    send_far(gated, 0)
 
     low = lax.broadcasted_iota(jnp.int32, (half, 2 * size), 1) < size
 
@@ -405,8 +401,7 @@
 
     add_far(0, end_first)
     start_halo(first, 1, (1,))
-    send_group(first, 1, 0, False, False)
-    send_rest(first, 1)
+    send_far(first, 1)
 
     for k in (10, 11):
         fetches[k].wait()

time: 26.4 us -> 24.9 us (0.943)
  Pallas kernels: 25.5 us -> 24.1 us
    pallas_call x1, Pallas kernels: 25.5 us -> 24.1 us  [local(): pl.pallas_call(functools.partial(kernel, n, ny), out_shape=jax.ShapeDtype...]
where the time goes in v7:
time: 24.9 us; the launch traced here: 24.8 us
  Pallas kernels  24.1 us (97%)
  local copies, waits for them, and re-layouts  0.71 us (3%)
    pallas_call x1, Pallas kernels, local(): pl.pallas_call(functools.partial(kernel, n, ny), out_shape=jax.ShapeDtype...  24.1 us
    unnamed x1, local copies, waits for them, and re-layouts  0.71 us

profile of v7, /device:TPU:0, one launch (start us, length us, event | category | flops | bytes accessed | tf_op | source)
XLA Modules:
  0.0 24.8 jit_solution(7916973329076149988)
XLA Ops:
  0.0 24.1 %shard_map.118 = bf16[4,4,64,128]{3,2,1,0:T(8,128)(2,1)S(1)} custom-call(bf16[4,4,64,128]{3,2,1,0:T(8,128)(2,1)} %refs_0_.1, bf16[2,32,32]{2,1,0:T(8,128)(2,1)} %refs_1_.1, bf16[2,32,32]{2,1,0:T(8,128)(2,1)} %refs_2_.1, f32[1,32]{1,0:T(1,128)} %bitcast.6, f32[1,32]{1,0:T(1,128)} %bitcast.7, bf16[4,5,4,4096]{3,2,1,0:T(4,128)(2,1)} %bitcast.5, ...), custom_call_target="tpu_custom_call" | custom-call | flops 167772160 | bytes 524288 | tf_op jit(solution)/shard_map/pallas_call | solution.py:520
  24.1 0.7 %copy.14 = bf16[4,4,64,128]{3,2,1,0:T(8,128)(2,1)} copy(bf16[4,4,64,128]{3,2,1,0:T(8,128)(2,1)S(1)} %shard_map.118) | data formatting | bytes 524288

commit v8 on v7

--- a/solution.py
+++ b/solution.py
@@ -211,8 +211,8 @@
     part = n // 2
 
     def destination(k):
-        side = (rx // part + 1 + k // part) % 2
-        return side * part + (rx % part + k % part + 1) % part
+        side = (rx // part + 1 + k % 2) % 2
+        return side * part + (rx % part + k // 2 + 1) % part
 
     lane = lax.broadcasted_iota(jnp.int32, (1, CAP * size), 1)
 

time: 24.9 us -> 23.7 us (0.952)
  Pallas kernels: 24.1 us -> 22.9 us
    pallas_call x1, Pallas kernels: 24.1 us -> 22.9 us  [local(): pl.pallas_call(functools.partial(kernel, n, ny), out_shape=jax.ShapeDtype...]
where the time goes in v8:
time: 23.7 us; the launch traced here: 23.6 us
  Pallas kernels  22.9 us (97%)
  local copies, waits for them, and re-layouts  0.71 us (3%)
    pallas_call x1, Pallas kernels, local(): pl.pallas_call(functools.partial(kernel, n, ny), out_shape=jax.ShapeDtype...  22.9 us
    unnamed x1, local copies, waits for them, and re-layouts  0.71 us

profile of v8, /device:TPU:0, one launch (start us, length us, event | category | flops | bytes accessed | tf_op | source)
XLA Modules:
  0.0 23.6 jit_solution(4620990937899955252)
XLA Ops:
  0.0 22.9 %shard_map.118 = bf16[4,4,64,128]{3,2,1,0:T(8,128)(2,1)S(1)} custom-call(bf16[4,4,64,128]{3,2,1,0:T(8,128)(2,1)} %refs_0_.1, bf16[2,32,32]{2,1,0:T(8,128)(2,1)} %refs_1_.1, bf16[2,32,32]{2,1,0:T(8,128)(2,1)} %refs_2_.1, f32[1,32]{1,0:T(1,128)} %bitcast.6, f32[1,32]{1,0:T(1,128)} %bitcast.7, bf16[4,5,4,4096]{3,2,1,0:T(4,128)(2,1)} %bitcast.5, ...), custom_call_target="tpu_custom_call" | custom-call | flops 167772160 | bytes 524288 | tf_op jit(solution)/shard_map/pallas_call | solution.py:520
  22.9 0.7 %copy.14 = bf16[4,4,64,128]{3,2,1,0:T(8,128)(2,1)} copy(bf16[4,4,64,128]{3,2,1,0:T(8,128)(2,1)S(1)} %shard_map.118) | data formatting | bytes 524288

commit v9 on v8

--- a/solution.py
+++ b/solution.py
@@ -263,7 +263,7 @@
             target_send[d] = named
             target_copy(d, rx).start()
 
-    team = 4
+    team = 2
 
     def send_group(signal, hop, start, last):
         ks = [start + g for g in range(team)]

time: 23.7 us -> 23.6 us (level)
  no operation moved by 1% of the time
where the time goes in v9:
time: 23.6 us; the launch traced here: 23.4 us
  Pallas kernels  22.7 us (96%)
  local copies, waits for them, and re-layouts  0.71 us (3%)
    pallas_call x1, Pallas kernels, local(): pl.pallas_call(functools.partial(kernel, n, ny), out_shape=jax.ShapeDtype...  22.7 us
    unnamed x1, local copies, waits for them, and re-layouts  0.71 us

profile of v9, /device:TPU:0, one launch (start us, length us, event | category | flops | bytes accessed | tf_op | source)
XLA Modules:
  0.0 23.4 jit_solution(13830425897351982637)
XLA Ops:
  0.0 22.7 %shard_map.118 = bf16[4,4,64,128]{3,2,1,0:T(8,128)(2,1)S(1)} custom-call(bf16[4,4,64,128]{3,2,1,0:T(8,128)(2,1)} %refs_0_.1, bf16[2,32,32]{2,1,0:T(8,128)(2,1)} %refs_1_.1, bf16[2,32,32]{2,1,0:T(8,128)(2,1)} %refs_2_.1, f32[1,32]{1,0:T(1,128)} %bitcast.6, f32[1,32]{1,0:T(1,128)} %bitcast.7, bf16[4,5,4,4096]{3,2,1,0:T(4,128)(2,1)} %bitcast.5, ...), custom_call_target="tpu_custom_call" | custom-call | flops 167772160 | bytes 524288 | tf_op jit(solution)/shard_map/pallas_call | solution.py:520
  22.7 0.7 %copy.14 = bf16[4,4,64,128]{3,2,1,0:T(8,128)(2,1)} copy(bf16[4,4,64,128]{3,2,1,0:T(8,128)(2,1)S(1)} %shard_map.118) | data formatting | bytes 524288
